TPU v7x, 512 devices: a whole 4x8x8 slice. The times are simulated.
512 devices in a mesh: dp: 64 (over z, y_lo, core), tensor: 8 (over x, y_hi).
Axes of the slice: x: 4, y: 8 (y_hi: 2, y_lo: 4; y = y_hi * 4 + y_lo), z: 8, core: 2. Of those that a mesh axis runs over, the one named last changes fastest.
Arguments:
- queries: bfloat16 [32768, 8192], P(('dp', 'tensor')), may hold values from -160 to 160
- key_rows: bfloat16 [32768, 1024], P(('dp', 'tensor')), may hold values from -6 to 6
- value_rows_initial: bfloat16 [32768, 1024], P(('dp', 'tensor')), may hold values from -6 to 6
- grad_out: bfloat16 [32768, 8192], P('dp', 'tensor'), may hold values from -6 to 6
- seg_ids: int32 [64, 512], replicated, may hold values from 0 to 8, as said below
- pair_mask: int32 [64], replicated, may hold values from 0 to 63, as said below
- sender: int32 [64], replicated, may hold values from 0 to 1, as said below
- moved_seq: int32 [64], replicated, may hold values from 0 to 7, as said below
Outputs:
- attn_out: bfloat16 [32768, 8192], P('dp', 'tensor')
- grad_queries: bfloat16 [32768, 8192], P(('dp', 'tensor'))
- grad_keys: bfloat16 [32768, 1024], P(('dp', 'tensor'))
- grad_values: bfloat16 [32768, 1024], P(('dp', 'tensor'))
Inputs may be any that keep to these rules, and one draw needn't show every extreme that they name: `seg_ids`: each row is non-decreasing: every label 0 to 7 is used by a run of slots, then 8 fills the unused slots. `pair_mask`: entry g is g XOR m for one m of 1 to 63 common to all groups (so m is entry 0). `sender`: exactly one group of every pair has 1. A giving group's sequence moved_seq has at most 128 rows, exactly 128 for some group; a receiving group uses at most 384 slots, exactly that many for some group; some giving group uses all 512. `moved_seq`: read only for giving groups.
All inputs are finite; a program needn't handle non-finite values.
Results may differ from a plain program's by a relative error of at most 0.0091.
Values may be sent and summed in bfloat16 or wider, within the bound.
No kernel may reach another device: no remote copies, remote signals or barrier semaphores. Data moves between devices by JAX's collectives and lax.ppermute only.
A program may use at most 128 MiB of HBM per device.

v0:
```python
import jax
import jax.numpy as jnp
from jax import lax
from jax.sharding import PartitionSpec as P

HEAD_DIMENSION = 128
SEQS = 8
MOVE = 128


def swapped_2(block, axis, distance):
    count = lax.axis_size(axis)
    route = []
    for low in range(count):
        high = low | 1 << distance
        if high != low and high < count:
            route += [(low, high), (high, low)]
    return lax.ppermute(block, axis, route)


def head_pass(query_head, key_head, value_head, grad_head, allowed, live_rows, factor):
    scores = jnp.dot(query_head, key_head.T, preferred_element_type=jnp.float32) * factor
    scores = jnp.where(allowed, scores, jnp.float32(-1e30))
    row_peak = jnp.max(scores, axis=1, keepdims=True)
    weights = jnp.exp(scores - row_peak)
    softmax_rows = weights / jnp.sum(weights, axis=1, keepdims=True)
    probs_low = softmax_rows.astype(jnp.bfloat16)
    output = jnp.dot(probs_low, value_head, preferred_element_type=jnp.float32)
    output = jnp.where(live_rows[:, None], output, jnp.zeros_like(output)).astype(jnp.bfloat16)
    grad_live = jnp.where(live_rows[:, None], grad_head, jnp.zeros_like(grad_head))
    grad_value = jnp.dot(probs_low.T, grad_live, preferred_element_type=jnp.float32)
    grad_probs = jnp.dot(grad_live, value_head.T, preferred_element_type=jnp.float32)
    center = jnp.sum(
        grad_live.astype(jnp.float32) * output.astype(jnp.float32), axis=1, keepdims=True
    )
    grad_scores = (softmax_rows * (grad_probs - center)).astype(jnp.bfloat16)
    grad_query = (
        jnp.dot(grad_scores, key_head, preferred_element_type=jnp.float32) * factor
    ).astype(jnp.bfloat16)
    grad_key = jnp.dot(grad_scores.T, query_head, preferred_element_type=jnp.float32) * factor
    return (output, grad_query, grad_key, grad_value)


def attend_block(updated_rows, sequence_labels, grad_rows, heads_q, heads_kv, head_size):
    count_rows = updated_rows.shape[0]
    query_cols = heads_q * head_size
    key_value_columns = heads_kv * head_size
    query_part = (
        updated_rows[:, :query_cols].reshape(count_rows, heads_q, head_size).transpose(1, 0, 2)
    )
    key_part = (
        updated_rows[:, query_cols : query_cols + key_value_columns]
        .reshape(count_rows, heads_kv, head_size)
        .transpose(1, 0, 2)
    )
    value_part = (
        updated_rows[:, query_cols + key_value_columns :]
        .reshape(count_rows, heads_kv, head_size)
        .transpose(1, 0, 2)
    )
    grad_part = grad_rows.reshape(count_rows, heads_q, head_size).transpose(1, 0, 2)
    positions = jnp.arange(count_rows, dtype=jnp.int32)
    live_rows = sequence_labels != SEQS
    allowed = (sequence_labels[:, None] == sequence_labels[None, :]) & live_rows[:, None] & (
        positions[None, :] <= positions[:, None]
    ) | (positions[:, None] == positions[None, :])
    group_size = heads_q // heads_kv
    factor = head_size ** (-0.5)

    def per_head(head_item):
        head_index, query_head, grad_head = head_item
        kv_index = head_index // group_size
        key_head = lax.dynamic_index_in_dim(key_part, kv_index, 0, keepdims=False)
        value_head = lax.dynamic_index_in_dim(value_part, kv_index, 0, keepdims=False)
        return head_pass(query_head, key_head, value_head, grad_head, allowed, live_rows, factor)

    outputs, grad_query, grad_key, grad_value = lax.map(
        per_head, (jnp.arange(heads_q, dtype=jnp.int32), query_part, grad_part)
    )
    attention = outputs.transpose(1, 0, 2).reshape(count_rows, query_cols)
    grad_key = (
        grad_key.reshape(heads_kv, group_size, count_rows, head_size)
        .sum(axis=1)
        .astype(jnp.bfloat16)
    )
    grad_value = (
        grad_value.reshape(heads_kv, group_size, count_rows, head_size)
        .sum(axis=1)
        .astype(jnp.bfloat16)
    )
    gradients = jnp.concatenate(
        [
            grad_query.transpose(1, 0, 2).reshape(count_rows, query_cols),
            grad_key.transpose(1, 0, 2).reshape(count_rows, key_value_columns),
            grad_value.transpose(1, 0, 2).reshape(count_rows, key_value_columns),
        ],
        axis=1,
    )
    return (attention, gradients)


def carry_rows(packet, xor_value, bit_count):
    bit_order = list(range(bit_count))
    for bit_index in bit_order:
        bit_set = jnp.bitwise_and(jnp.right_shift(xor_value, bit_index), 1) == 1
        swapped = swapped_2(packet, "dp", bit_index)
        packet = jnp.where(bit_set, swapped, packet)
    return packet


def on_device(
    queries, key_rows, value_rows_initial, grad_out, seg_ids, pair_mask, sender, moved_seq
):
    query_local, key_local, value_local = (
        lax.all_to_all(queries, "tensor", split_axis=1, concat_axis=0, tiled=True),
        lax.all_to_all(key_rows, "tensor", split_axis=1, concat_axis=0, tiled=True),
        lax.all_to_all(value_rows_initial, "tensor", split_axis=1, concat_axis=0, tiled=True),
    )
    count_rows = query_local.shape[0]
    heads_q = query_local.shape[1] // HEAD_DIMENSION
    heads_kv = key_local.shape[1] // HEAD_DIMENSION
    query_cols = query_local.shape[1]
    key_value_columns = key_local.shape[1]
    rows_own = jnp.concatenate([query_local, key_local, value_local], axis=1)
    row_width = rows_own.shape[1]
    group_position_index = lax.axis_index("dp")
    xor_value = pair_mask[0]
    partner_index = jnp.bitwise_xor(group_position_index, xor_value)
    live_all = jnp.sum(seg_ids < SEQS, axis=1)
    start_all = jnp.sum(seg_ids < moved_seq[:, None], axis=1)
    count_all = jnp.sum(seg_ids == moved_seq[:, None], axis=1)
    live_here = live_all[group_position_index]
    start_here = start_all[group_position_index]
    bit_count = lax.axis_size("dp").bit_length() - 1
    padded = jnp.concatenate([rows_own, jnp.zeros((MOVE, row_width), jnp.bfloat16)], axis=0)
    packet = lax.dynamic_slice_in_dim(padded, start_here, MOVE, 0)
    packet = carry_rows(packet, xor_value, bit_count)
    placed = lax.dynamic_update_slice_in_dim(padded, packet, live_here, 0)[:count_rows]
    positions = jnp.arange(count_rows, dtype=jnp.int32)
    giving = sender[group_position_index] == 1
    own_labels = seg_ids[group_position_index]
    moved_label = moved_seq[group_position_index]
    sequence_labels = jnp.where(
        giving,
        jnp.where(own_labels == moved_label, SEQS, own_labels),
        jnp.where(
            positions < live_here,
            own_labels,
            jnp.where(positions < live_here + count_all[partner_index], SEQS + 1, SEQS),
        ),
    )
    updated_rows = jnp.where(giving, rows_own, placed)
    attention, gradients = attend_block(
        updated_rows, sequence_labels, grad_out, heads_q, heads_kv, HEAD_DIMENSION
    )
    returning = lax.dynamic_slice_in_dim(gradients, live_here, MOVE, 0)
    returning = carry_rows(returning, xor_value, bit_count)
    back_placed = lax.dynamic_update_slice_in_dim(
        jnp.zeros((count_rows + MOVE, row_width), jnp.bfloat16), returning, start_here, 0
    )[:count_rows]
    handed = jnp.where((own_labels == moved_label)[:, None], back_placed, gradients)
    kept = jnp.where((positions < live_here)[:, None], gradients, jnp.zeros_like(gradients))
    restored = jnp.where(giving, handed, kept)
    grad_query = restored[:, :query_cols]
    grad_key = restored[:, query_cols : query_cols + key_value_columns]
    grad_value = restored[:, query_cols + key_value_columns :]
    grad_query, grad_key, grad_value = (
        lax.all_to_all(grad_query, "tensor", split_axis=0, concat_axis=1, tiled=True),
        lax.all_to_all(grad_key, "tensor", split_axis=0, concat_axis=1, tiled=True),
        lax.all_to_all(grad_value, "tensor", split_axis=0, concat_axis=1, tiled=True),
    )
    return (attention, grad_query, grad_key, grad_value)


def solution(mesh):
    return jax.shard_map(
        on_device,
        mesh=mesh,
        in_specs=(
            P(("dp", "tensor"), None),
            P(("dp", "tensor"), None),
            P(("dp", "tensor"), None),
            P("dp", "tensor"),
            P(),
            P(),
            P(),
            P(),
        ),
        out_specs=(
            P("dp", "tensor"),
            P(("dp", "tensor"), None),
            P(("dp", "tensor"), None),
            P(("dp", "tensor"), None),
        ),
        check_vma=False,
    )
```

profile of v0, /device:TPU:1, one launch (start us, length us, event | category | flops | bytes accessed | tf_op | source)
XLA Modules:
  0.0 355.8 jit_solution(1126270748572531585)
XLA Ops:
  2.2 10.1 %all-to-all-start.2 = ((bf16[64,8,128]{2,0,1:T(8,128)(2,1)}), bf16[64,8,128]{2,0,1:T(8,128)(2,1)S(1)}, u32[]{:S(2)}, u32[]{:S(2)}) async-start(bf16[64,8,128]{2,0,1:T(8,128)(2,1)} %copy_bitcast_fusion.3), calls=%async_computation.2 | async-start | bytes 262144 | tf_op jit(solution)/shard_map/all_to_all | solution.py:117
  13.9 8.0 %all-to-all-done.2 = bf16[64,8,128]{2,0,1:T(8,128)(2,1)S(1)} async-done(((bf16[64,8,128]{2,0,1:T(8,128)(2,1)}), bf16[64,8,128]{2,0,1:T(8,128)(2,1)S(1)}, u32[]{:S(2)}, u32[]{:S(2)}) %all-to-all-start.2) | async-done | bytes 131104 | tf_op jit(solution)/shard_map/all_to_all | solution.py:117
  26.4 8.3 %all-to-all-done.1 = bf16[64,8,128]{2,0,1:T(8,128)(2,1)S(1)} async-done(((bf16[64,8,128]{2,0,1:T(8,128)(2,1)}), bf16[64,8,128]{2,0,1:T(8,128)(2,1)S(1)}, u32[]{:S(2)}, u32[]{:S(2)}) %all-to-all-start.1) | async-done | bytes 131104 | tf_op jit(solution)/shard_map/all_to_all | solution.py:116
  41.0 17.6 %all-to-all-done = bf16[64,8,1024]{2,0,1:T(8,128)(2,1)S(1)} async-done(((bf16[64,8,1024]{2,0,1:T(8,128)(2,1)}), bf16[64,8,1024]{2,0,1:T(8,128)(2,1)S(1)}, u32[]{:S(2)}, u32[]{:S(2)}) %all-to-all-start) | async-done | bytes 1048608 | tf_op jit(solution)/shard_map/all_to_all | solution.py:115
  58.9 7.8 %collective-permute-start = (bf16[128,1280]{1,0:T(8,128)(2,1)S(1)}, bf16[128,1280]{1,0:T(8,128)(2,1)S(1)}, u32[]{:S(2)}, u32[]{:S(2)}) collective-permute-start(bf16[128,1280]{1,0:T(8,128)(2,1)S(1)} %constant_dynamic-slice_fusion.1), channel_id=1, source_target_pairs={{0,8},{8,0},{16,24},{24,16},{32,40},{40,32},{48,56},{56,48},{64,72... | collective-permute-start | bytes 983048 | tf_op jit(solution)/shard_map/ppermute | solution.py:18
  68.1 8.0 %collective-permute-start.1 = (bf16[128,1280]{1,0:T(8,128)(2,1)S(1)}, bf16[128,1280]{1,0:T(8,128)(2,1)S(1)}, u32[]{:S(2)}, u32[]{:S(2)}) collective-permute-start(bf16[128,1280]{1,0:T(8,128)(2,1)S(1)} %broadcast_select_fusion.1), channel_id=1, source_target_pairs={{0,16},{16,0},{8,24},{24,8},{32,48},{48,32},{40,56},{56,40},{64,80... | collective-permute-start | bytes 983048 | tf_op jit(solution)/shard_map/ppermute | solution.py:18
  76.1 7.7 %collective-permute-done.1 = bf16[128,1280]{1,0:T(8,128)(2,1)S(1)} collective-permute-done((bf16[128,1280]{1,0:T(8,128)(2,1)S(1)}, bf16[128,1280]{1,0:T(8,128)(2,1)S(1)}, u32[]{:S(2)}, u32[]{:S(2)}) %collective-permute-start.1) | collective-permute-done | bytes 327712 | tf_op jit(solution)/shard_map/ppermute | solution.py:18
  86.8 15.7 %collective-permute-done.2 = bf16[128,1280]{1,0:T(8,128)(2,1)S(1)} collective-permute-done((bf16[128,1280]{1,0:T(8,128)(2,1)S(1)}, bf16[128,1280]{1,0:T(8,128)(2,1)S(1)}, u32[]{:S(2)}, u32[]{:S(2)}) %collective-permute-start.2) | collective-permute-done | bytes 327712 | tf_op jit(solution)/shard_map/ppermute | solution.py:18
  106.5 6.6 %collective-permute-done.3 = bf16[128,1280]{1,0:T(8,128)(2,1)S(1)} collective-permute-done((bf16[128,1280]{1,0:T(8,128)(2,1)S(1)}, bf16[128,1280]{1,0:T(8,128)(2,1)S(1)}, u32[]{:S(2)}, u32[]{:S(2)}) %collective-permute-start.3) | collective-permute-done | bytes 327712 | tf_op jit(solution)/shard_map/ppermute | solution.py:18
  113.9 5.8 %collective-permute-start.4 = (bf16[128,1280]{1,0:T(8,128)(2,1)}, bf16[128,1280]{1,0:T(8,128)(2,1)}, u32[]{:S(2)}, u32[]{:S(2)}) collective-permute-start(bf16[128,1280]{1,0:T(8,128)(2,1)} %broadcast_select_fusion.7), channel_id=1, source_target_pairs={{0,128},{128,0},{8,136},{136,8},{16,144},{144,16},{24,152},{152,24... | collective-permute-start | bytes 983048 | tf_op jit(solution)/shard_map/ppermute | solution.py:18
  128.7 5.5 %collective-permute-done.4 = bf16[128,1280]{1,0:T(8,128)(2,1)} collective-permute-done((bf16[128,1280]{1,0:T(8,128)(2,1)}, bf16[128,1280]{1,0:T(8,128)(2,1)}, u32[]{:S(2)}, u32[]{:S(2)}) %collective-permute-start.4) | collective-permute-done | bytes 327712 | tf_op jit(solution)/shard_map/ppermute | solution.py:18
  135.2 8.2 %collective-permute-start.5 = (bf16[128,1280]{1,0:T(8,128)(2,1)S(1)}, bf16[128,1280]{1,0:T(8,128)(2,1)S(1)}, u32[]{:S(2)}, u32[]{:S(2)}) collective-permute-start(bf16[128,1280]{1,0:T(8,128)(2,1)S(1)} %broadcast_select_fusion.9), channel_id=1, source_target_pairs={{0,256},{256,0},{8,264},{264,8},{16,272},{272,16},{24,280},{280,24... | collective-permute-start | bytes 983048 | tf_op jit(solution)/shard_map/ppermute | solution.py:18
  148.0 7.9 %collective-permute-done.5 = bf16[128,1280]{1,0:T(8,128)(2,1)S(1)} collective-permute-done((bf16[128,1280]{1,0:T(8,128)(2,1)S(1)}, bf16[128,1280]{1,0:T(8,128)(2,1)S(1)}, u32[]{:S(2)}, u32[]{:S(2)}) %collective-permute-start.5) | collective-permute-done | bytes 327712 | tf_op jit(solution)/shard_map/ppermute | solution.py:18
  161.3 41.6 %while.19 = (s32[]{:T(128)}, bf16[8,512,128]{1,2,0:T(8,128)(2,1)}, bf16[8,512,128]{1,2,0:T(8,128)(2,1)}, f32[8,512,128]{2,1,0:T(8,128)}, f32[8,512,128]{2,1,0:T(...) while((s32[]{:T(128)}, bf16[8,512,128]{1,2,0:T(8,128)(2,1)}, ...), condition=%wide.region_7.8_spmd.clone.clone, body=%wide.region_3.7_spmd.clone.clone.sunk | while | flops 409205248 | bytes 10124965 | solution.py:77
  206.8 5.2 %collective-permute-start.6 = (bf16[128,1280]{1,0:T(8,128)(2,1)S(1)}, bf16[128,1280]{1,0:T(8,128)(2,1)S(1)}, u32[]{:S(2)}, u32[]{:S(2)}) collective-permute-start(bf16[128,1280]{1,0:T(8,128)(2,1)S(1)} %constant_dynamic-slice_fusion), channel_id=1, source_target_pairs={{0,8},{8,0},{16,24},{24,16},{32,40},{40,32},{48,56},{56,48},{64,72... | collective-permute-start | bytes 983048 | tf_op jit(solution)/shard_map/ppermute | solution.py:18
  215.3 8.9 %collective-permute-done.7 = bf16[128,1280]{1,0:T(8,128)(2,1)S(1)} collective-permute-done((bf16[128,1280]{1,0:T(8,128)(2,1)S(1)}, bf16[128,1280]{1,0:T(8,128)(2,1)S(1)}, u32[]{:S(2)}, u32[]{:S(2)}) %collective-permute-start.7) | collective-permute-done | bytes 327712 | tf_op jit(solution)/shard_map/ppermute | solution.py:18
  226.3 17.4 %collective-permute-done.8 = bf16[128,1280]{1,0:T(8,128)(2,1)S(1)} collective-permute-done((bf16[128,1280]{1,0:T(8,128)(2,1)S(1)}, bf16[128,1280]{1,0:T(8,128)(2,1)S(1)}, u32[]{:S(2)}, u32[]{:S(2)}) %collective-permute-start.8) | collective-permute-done | bytes 327712 | tf_op jit(solution)/shard_map/ppermute | solution.py:18
  245.6 8.7 %collective-permute-done.9 = bf16[128,1280]{1,0:T(8,128)(2,1)S(1)} collective-permute-done((bf16[128,1280]{1,0:T(8,128)(2,1)S(1)}, bf16[128,1280]{1,0:T(8,128)(2,1)S(1)}, u32[]{:S(2)}, u32[]{:S(2)}) %collective-permute-start.9) | collective-permute-done | bytes 327712 | tf_op jit(solution)/shard_map/ppermute | solution.py:18
  254.4 5.0 %collective-permute-start.10 = (bf16[128,1280]{1,0:T(8,128)(2,1)S(1)}, bf16[128,1280]{1,0:T(8,128)(2,1)S(1)}, u32[]{:S(2)}, u32[]{:S(2)}) collective-permute-start(bf16[128,1280]{1,0:T(8,128)(2,1)S(1)} %broadcast_select_fusion.6), channel_id=1, source_target_pairs={{0,128},{128,0},{8,136},{136,8},{16,144},{144,16},{24,152},{152,24... | collective-permute-start | bytes 983048 | tf_op jit(solution)/shard_map/ppermute | solution.py:18
  259.4 14.3 %collective-permute-done.10 = bf16[128,1280]{1,0:T(8,128)(2,1)S(1)} collective-permute-done((bf16[128,1280]{1,0:T(8,128)(2,1)S(1)}, bf16[128,1280]{1,0:T(8,128)(2,1)S(1)}, u32[]{:S(2)}, u32[]{:S(2)}) %collective-permute-start.10) | collective-permute-done | bytes 327712 | tf_op jit(solution)/shard_map/ppermute | solution.py:18
  278.8 16.8 %collective-permute-done.11 = bf16[128,1280]{1,0:T(8,128)(2,1)S(1)} collective-permute-done((bf16[128,1280]{1,0:T(8,128)(2,1)S(1)}, bf16[128,1280]{1,0:T(8,128)(2,1)S(1)}, u32[]{:S(2)}, u32[]{:S(2)}) %collective-permute-start.11) | collective-permute-done | bytes 327712 | tf_op jit(solution)/shard_map/ppermute | solution.py:18
  300.3 11.8 %all_to_all.114 = bf16[8,64,128]{2,1,0:T(8,128)(2,1)S(1)} all-to-all(bf16[8,64,128]{2,1,0:T(8,128)(2,1)S(1)} %bitcast.155), channel_id=1, replica_groups=mesh['dp'=64,'tensor'=8] {'tensor'}, dimensions={0} | all-to-all | bytes 262144 | tf_op jit(solution)/shard_map/all_to_all | solution.py:170
  317.9 7.1 %all-to-all-done.4 = bf16[8,64,128]{2,1,0:T(8,128)(2,1)S(1)} async-done(((bf16[8,64,128]{2,1,0:T(8,128)(2,1)}), bf16[8,64,128]{2,1,0:T(8,128)(2,1)S(1)}, u32[]{:S(2)}, u32[]{:S(2)}) %all-to-all-start.4) | async-done | bytes 131104 | tf_op jit(solution)/shard_map/all_to_all | solution.py:169
  331.2 23.5 %all-to-all-done.3 = bf16[8,64,1024]{2,1,0:T(8,128)(2,1)S(1)} async-done(((bf16[8,64,1024]{2,1,0:T(8,128)(2,1)}), bf16[8,64,1024]{2,1,0:T(8,128)(2,1)S(1)}, u32[]{:S(2)}, u32[]{:S(2)}) %all-to-all-start.3) | async-done | bytes 1048608 | tf_op jit(solution)/shard_map/all_to_all | solution.py:168
  (184 shorter events, 111.5 us)
Async XLA Ops:
  0.6 24.6 %copy-start.7 = (bf16[64,8192]{1,0:T(8,128)(2,1)S(1)}, bf16[64,8192]{1,0:T(8,128)(2,1)}, u32[]{:S(2)}) copy-start(bf16[64,8192]{1,0:T(8,128)(2,1)} %param.10) | copy-start | bytes 3145732
  2.2 19.7 %all-to-all-start.2 = ((bf16[64,8,128]{2,0,1:T(8,128)(2,1)}), bf16[64,8,128]{2,0,1:T(8,128)(2,1)S(1)}, u32[]{:S(2)}, u32[]{:S(2)}) async-start(bf16[64,8,128]{2,0,1:T(8,128)(2,1)} %copy_bitcast_fusion.3), calls=%async_computation.2 | async-start | bytes 262144 | tf_op jit(solution)/shard_map/all_to_all | solution.py:117
  21.9 36.7 %copy-start.3 = (bf16[64,8,128]{2,0,1:T(8,128)(2,1)}, bf16[64,8,128]{2,0,1:T(8,128)(2,1)S(1)}, u32[]{:S(2)}) copy-start(bf16[64,8,128]{2,0,1:T(8,128)(2,1)S(1)} %all-to-all-done.2) | copy-start | bytes 393220
  21.9 12.8 %all-to-all-start.1 = ((bf16[64,8,128]{2,0,1:T(8,128)(2,1)}), bf16[64,8,128]{2,0,1:T(8,128)(2,1)S(1)}, u32[]{:S(2)}, u32[]{:S(2)}) async-start(bf16[64,8,128]{2,0,1:T(8,128)(2,1)} %copy_bitcast_fusion.4), calls=%async_computation.1 | async-start | bytes 262144 | tf_op jit(solution)/shard_map/all_to_all | solution.py:116
  25.3 12.9 %copy-start.9 = (s32[64,512]{1,0:T(8,128)S(1)}, s32[64,512]{1,0:T(8,128)}, u32[]{:S(2)}) copy-start(s32[64,512]{1,0:T(8,128)} %param.14) | copy-start | bytes 393220
  25.3 12.9 %copy-start.11 = (s32[64]{0:T(128)S(1)}, s32[64]{0:T(128)}, u32[]{:S(2)}) copy-start(s32[64]{0:T(128)} %param.17) | copy-start | bytes 772
  34.7 24.1 %copy-start.5 = (bf16[64,8,128]{2,0,1:T(8,128)(2,1)}, bf16[64,8,128]{2,0,1:T(8,128)(2,1)S(1)}, u32[]{:S(2)}) copy-start(bf16[64,8,128]{2,0,1:T(8,128)(2,1)S(1)} %all-to-all-done.1) | copy-start | bytes 393220
  34.7 24.0 %all-to-all-start = ((bf16[64,8,1024]{2,0,1:T(8,128)(2,1)}), bf16[64,8,1024]{2,0,1:T(8,128)(2,1)S(1)}, u32[]{:S(2)}, u32[]{:S(2)}) async-start(bf16[64,8,1024]{2,0,1:T(8,128)(2,1)} %bitcast.111), calls=%async_computation | async-start | bytes 2097152 | tf_op jit(solution)/shard_map/all_to_all | solution.py:115
  58.9 9.1 %collective-permute-start = (bf16[128,1280]{1,0:T(8,128)(2,1)S(1)}, bf16[128,1280]{1,0:T(8,128)(2,1)S(1)}, u32[]{:S(2)}, u32[]{:S(2)}) collective-permute-start(bf16[128,1280]{1,0:T(8,128)(2,1)S(1)} %constant_dynamic-slice_fusion.1), channel_id=1, source_target_pairs={{0,8},{8,0},{16,24},{24,16},{32,40},{40,32},{48,56},{56,48},{64,72... | collective-permute-start | bytes 983048 | tf_op jit(solution)/shard_map/ppermute | solution.py:18
  68.1 54.2 %copy-start.13 = (s32[64]{0:T(128)S(1)}, s32[64]{0:T(128)}, u32[]{:S(2)}) copy-start(s32[64]{0:T(128)} %param.16) | copy-start | bytes 772
  68.1 15.7 %collective-permute-start.1 = (bf16[128,1280]{1,0:T(8,128)(2,1)S(1)}, bf16[128,1280]{1,0:T(8,128)(2,1)S(1)}, u32[]{:S(2)}, u32[]{:S(2)}) collective-permute-start(bf16[128,1280]{1,0:T(8,128)(2,1)S(1)} %broadcast_select_fusion.1), channel_id=1, source_target_pairs={{0,16},{16,0},{8,24},{24,8},{32,48},{48,32},{40,56},{56,40},{64,80... | collective-permute-start | bytes 983048 | tf_op jit(solution)/shard_map/ppermute | solution.py:18
  83.9 18.5 %collective-permute-start.2 = (bf16[128,1280]{1,0:T(8,128)(2,1)S(1)}, bf16[128,1280]{1,0:T(8,128)(2,1)S(1)}, u32[]{:S(2)}, u32[]{:S(2)}) collective-permute-start(bf16[128,1280]{1,0:T(8,128)(2,1)S(1)} %broadcast_select_fusion.3), channel_id=1, source_target_pairs={{0,32},{32,0},{8,40},{40,8},{16,48},{48,16},{24,56},{56,24},{64,96... | collective-permute-start | bytes 983048 | tf_op jit(solution)/shard_map/ppermute | solution.py:18
  102.5 10.6 %collective-permute-start.3 = (bf16[128,1280]{1,0:T(8,128)(2,1)S(1)}, bf16[128,1280]{1,0:T(8,128)(2,1)S(1)}, u32[]{:S(2)}, u32[]{:S(2)}) collective-permute-start(bf16[128,1280]{1,0:T(8,128)(2,1)S(1)} %broadcast_select_fusion.5), channel_id=1, source_target_pairs={{0,64},{64,0},{8,72},{72,8},{16,80},{80,16},{24,88},{88,24},{32,96... | collective-permute-start | bytes 983048 | tf_op jit(solution)/shard_map/ppermute | solution.py:18
  113.9 20.3 %collective-permute-start.4 = (bf16[128,1280]{1,0:T(8,128)(2,1)}, bf16[128,1280]{1,0:T(8,128)(2,1)}, u32[]{:S(2)}, u32[]{:S(2)}) collective-permute-start(bf16[128,1280]{1,0:T(8,128)(2,1)} %broadcast_select_fusion.7), channel_id=1, source_target_pairs={{0,128},{128,0},{8,136},{136,8},{16,144},{144,16},{24,152},{152,24... | collective-permute-start | bytes 983048 | tf_op jit(solution)/shard_map/ppermute | solution.py:18
  135.2 20.7 %collective-permute-start.5 = (bf16[128,1280]{1,0:T(8,128)(2,1)S(1)}, bf16[128,1280]{1,0:T(8,128)(2,1)S(1)}, u32[]{:S(2)}, u32[]{:S(2)}) collective-permute-start(bf16[128,1280]{1,0:T(8,128)(2,1)S(1)} %broadcast_select_fusion.9), channel_id=1, source_target_pairs={{0,256},{256,0},{8,264},{264,8},{16,272},{272,16},{24,280},{280,24... | collective-permute-start | bytes 983048 | tf_op jit(solution)/shard_map/ppermute | solution.py:18
  206.8 6.4 %collective-permute-start.6 = (bf16[128,1280]{1,0:T(8,128)(2,1)S(1)}, bf16[128,1280]{1,0:T(8,128)(2,1)S(1)}, u32[]{:S(2)}, u32[]{:S(2)}) collective-permute-start(bf16[128,1280]{1,0:T(8,128)(2,1)S(1)} %constant_dynamic-slice_fusion), channel_id=1, source_target_pairs={{0,8},{8,0},{16,24},{24,16},{32,40},{40,32},{48,56},{56,48},{64,72... | collective-permute-start | bytes 983048 | tf_op jit(solution)/shard_map/ppermute | solution.py:18
  213.4 10.8 %collective-permute-start.7 = (bf16[128,1280]{1,0:T(8,128)(2,1)S(1)}, bf16[128,1280]{1,0:T(8,128)(2,1)S(1)}, u32[]{:S(2)}, u32[]{:S(2)}) collective-permute-start(bf16[128,1280]{1,0:T(8,128)(2,1)S(1)} %broadcast_select_fusion), channel_id=1, source_target_pairs={{0,16},{16,0},{8,24},{24,8},{32,48},{48,32},{40,56},{56,40},{64,80... | collective-permute-start | bytes 983048 | tf_op jit(solution)/shard_map/ppermute | solution.py:18
  224.3 19.4 %collective-permute-start.8 = (bf16[128,1280]{1,0:T(8,128)(2,1)S(1)}, bf16[128,1280]{1,0:T(8,128)(2,1)S(1)}, u32[]{:S(2)}, u32[]{:S(2)}) collective-permute-start(bf16[128,1280]{1,0:T(8,128)(2,1)S(1)} %broadcast_select_fusion.2), channel_id=1, source_target_pairs={{0,32},{32,0},{8,40},{40,8},{16,48},{48,16},{24,56},{56,24},{64,96... | collective-permute-start | bytes 983048 | tf_op jit(solution)/shard_map/ppermute | solution.py:18
  243.7 10.6 %collective-permute-start.9 = (bf16[128,1280]{1,0:T(8,128)(2,1)S(1)}, bf16[128,1280]{1,0:T(8,128)(2,1)S(1)}, u32[]{:S(2)}, u32[]{:S(2)}) collective-permute-start(bf16[128,1280]{1,0:T(8,128)(2,1)S(1)} %broadcast_select_fusion.4), channel_id=1, source_target_pairs={{0,64},{64,0},{8,72},{72,8},{16,80},{80,16},{24,88},{88,24},{32,96... | collective-permute-start | bytes 983048 | tf_op jit(solution)/shard_map/ppermute | solution.py:18
  254.4 19.3 %collective-permute-start.10 = (bf16[128,1280]{1,0:T(8,128)(2,1)S(1)}, bf16[128,1280]{1,0:T(8,128)(2,1)S(1)}, u32[]{:S(2)}, u32[]{:S(2)}) collective-permute-start(bf16[128,1280]{1,0:T(8,128)(2,1)S(1)} %broadcast_select_fusion.6), channel_id=1, source_target_pairs={{0,128},{128,0},{8,136},{136,8},{16,144},{144,16},{24,152},{152,24... | collective-permute-start | bytes 983048 | tf_op jit(solution)/shard_map/ppermute | solution.py:18
  273.7 21.8 %collective-permute-start.11 = (bf16[128,1280]{1,0:T(8,128)(2,1)S(1)}, bf16[128,1280]{1,0:T(8,128)(2,1)S(1)}, u32[]{:S(2)}, u32[]{:S(2)}) collective-permute-start(bf16[128,1280]{1,0:T(8,128)(2,1)S(1)} %broadcast_select_fusion.8), channel_id=1, source_target_pairs={{0,256},{256,0},{8,264},{264,8},{16,272},{272,16},{24,280},{280,24... | collective-permute-start | bytes 983048 | tf_op jit(solution)/shard_map/ppermute | solution.py:18
  312.2 12.9 %all-to-all-start.4 = ((bf16[8,64,128]{2,1,0:T(8,128)(2,1)}), bf16[8,64,128]{2,1,0:T(8,128)(2,1)S(1)}, u32[]{:S(2)}, u32[]{:S(2)}) async-start(bf16[8,64,128]{2,1,0:T(8,128)(2,1)} %bitcast.25), calls=%async_computation.4 | async-start | bytes 262144 | tf_op jit(solution)/shard_map/all_to_all | solution.py:169
  315.5 13.0 %copy-start.8 = (bf16[8,512,128]{1,2,0:T(8,128)(2,1)S(1)}, bf16[8,512,128]{1,2,0:T(8,128)(2,1)}, u32[]{:S(2)}) copy-start(bf16[8,512,128]{1,2,0:T(8,128)(2,1)} %get-tuple-element.90) | copy-start | bytes 3145732
  325.0 29.7 %all-to-all-start.3 = ((bf16[8,64,1024]{2,1,0:T(8,128)(2,1)}), bf16[8,64,1024]{2,1,0:T(8,128)(2,1)S(1)}, u32[]{:S(2)}, u32[]{:S(2)}) async-start(bf16[8,64,1024]{2,1,0:T(8,128)(2,1)} %bitcast.23), calls=%async_computation.3 | async-start | bytes 2097152 | tf_op jit(solution)/shard_map/all_to_all | solution.py:168
  (14 other events, 42.0 us)
where the time goes:
time: 357 us; the launch traced here: 356 us
  waiting for transfers between devices  176 us (49%)
  starting transfers between devices  81 us (23%)
  matrix products  32.9 us (9%)
  local copies, waits for them, and re-layouts  32.1 us (9%)
  other arithmetic  13.1 us (4%)
  blocking collectives  11.8 us (3%)
  between operations  8.16 us (2%)
    ppermute x12, waiting for transfers between devices, swapped_2(): return lax.ppermute(block, axis, route)  112 us
    ppermute x12, starting transfers between devices, swapped_2(): return lax.ppermute(block, axis, route)  57.1 us
    all_to_all x1, waiting for transfers between devices, on_device(): lax.all_to_all(grad_query, 'tensor', split_axis=0, concat_axis=1, tiled=T...  23.5 us
    all_to_all x1, waiting for transfers between devices, on_device(): lax.all_to_all(queries, 'tensor', split_axis=1, concat_axis=0, tiled=True)  17.6 us
    all_to_all x1, blocking collectives, on_device(): lax.all_to_all(grad_value, 'tensor', split_axis=0, concat_axis=1, tiled=T...  11.8 us
    all_to_all x1, starting transfers between devices, on_device(): lax.all_to_all(value_rows_initial, 'tensor', split_axis=1, concat_axis=0,...  10.1 us
    dot_general x8, matrix products, head_pass(): jnp.dot(probs_low.T, grad_live, preferred_element_type=jnp.float32)  8.33 us
    all_to_all x1, waiting for transfers between devices, on_device(): lax.all_to_all(key_rows, 'tensor', split_axis=1, concat_axis=0, tiled=True)  8.28 us
  transfers between devices with their start and end apart: 17, of which 17 were waited for; matrix products, arithmetic and copies ran while one was open for 5% of the time, Pallas kernels for 0%

commit v1 on v0

v1 whole, which is shorter than its diff:
```python
import functools

import jax
import jax.numpy as jnp
from jax import lax
from jax.experimental import pallas as pl
from jax.experimental.pallas import tpu as pltpu
from jax.sharding import PartitionSpec as P

HEAD = 128
SEQS = 8
MOVE = 128
FACTOR = HEAD**-0.5
LOG2E = 1.4426950408889634
BLOCKED = -1e30


def dot(a, b, contract_a, contract_b):
    return lax.dot_general(
        a, b, (((contract_a,), (contract_b,)), ((), ())), preferred_element_type=jnp.float32
    )


def attention_kernel(
    heads, tile, q_ref, k_ref, v_ref, g_ref, gt_ref, bias_ref, live_ref,
    o_ref, grads_ref, kt_ref, vt_ref, dk_ref, dv_ref,
):
    count_rows = k_ref.shape[0]
    head = pl.program_id(0)

    @pl.when(head == 0)
    def _():
        kt_ref[...] = k_ref[...].T
        vt_ref[...] = v_ref[...].T
        dk_ref[...] = jnp.zeros_like(dk_ref)
        dv_ref[...] = jnp.zeros_like(dv_ref)

    for first in range(0, count_rows, tile):
        seen = first + tile
        rows = pl.ds(first, tile)
        q = q_ref[rows, :]
        g = g_ref[rows, :]
        gt = gt_ref[:, rows]
        scores = dot(k_ref[:seen, :], q, 1, 1) + bias_ref[:seen, rows]
        peak = jnp.max(scores, axis=0, keepdims=True)
        weights = jnp.exp2((scores - peak) * (FACTOR * LOG2E))
        probs = weights * (1.0 / jnp.sum(weights, axis=0, keepdims=True))
        probs_low = probs.astype(jnp.bfloat16)
        out = dot(vt_ref[:, :seen], probs_low, 1, 0)
        out = (out * live_ref[:, rows]).astype(jnp.bfloat16)
        o_ref[rows, :] = out.T
        center = jnp.sum(
            gt.astype(jnp.float32) * out.astype(jnp.float32), axis=0, keepdims=True
        )
        grad_probs = dot(v_ref[:seen, :], gt, 1, 0)
        grad_scores = (probs * (grad_probs - center)).astype(jnp.bfloat16)
        grad_q = dot(kt_ref[:, :seen], grad_scores, 1, 0) * FACTOR
        columns = pl.ds(pl.multiple_of(head * HEAD, HEAD), HEAD)
        grads_ref[rows, columns] = grad_q.astype(jnp.bfloat16).T
        dk_ref[:seen, :] += dot(grad_scores, q, 1, 0)
        dv_ref[:seen, :] += dot(probs_low, g, 1, 0)

    @pl.when(head == heads - 1)
    def _():
        grads_ref[:, heads * HEAD : (heads + 1) * HEAD] = (dk_ref[...] * FACTOR).astype(
            jnp.bfloat16
        )
        grads_ref[:, (heads + 1) * HEAD :] = dv_ref[...].astype(jnp.bfloat16)


def attend(rows, grad, grad_t, bias, live, tile):
    count_rows, width = rows.shape
    heads = width // HEAD - 2
    block = lambda index: pl.BlockSpec((count_rows, HEAD), index)
    return pl.pallas_call(
        functools.partial(attention_kernel, heads, tile),
        grid=(heads,),
        in_specs=[
            block(lambda h: (0, h)),
            block(lambda h: (0, heads)),
            block(lambda h: (0, heads + 1)),
            block(lambda h: (0, h)),
            pl.BlockSpec((HEAD, count_rows), lambda h: (h, 0)),
            pl.BlockSpec((count_rows, count_rows), lambda h: (0, 0)),
            pl.BlockSpec((1, count_rows), lambda h: (0, 0)),
        ],
        out_specs=[
            block(lambda h: (0, h)),
            pl.BlockSpec((count_rows, width), lambda h: (0, 0)),
        ],
        out_shape=[
            jax.ShapeDtypeStruct((count_rows, heads * HEAD), jnp.bfloat16),
            jax.ShapeDtypeStruct((count_rows, width), jnp.bfloat16),
        ],
        scratch_shapes=[
            pltpu.VMEM((HEAD, count_rows), jnp.bfloat16),
            pltpu.VMEM((HEAD, count_rows), jnp.bfloat16),
            pltpu.VMEM((count_rows, HEAD), jnp.float32),
            pltpu.VMEM((count_rows, HEAD), jnp.float32),
        ],
        compiler_params=pltpu.CompilerParams(vmem_limit_bytes=24 * 2**20),
        cost_estimate=pl.CostEstimate(
            flops=12 * heads * count_rows * count_rows * HEAD,
            bytes_accessed=8 * 2**20,
            transcendentals=heads * count_rows * count_rows,
        ),
        name="attention",
    )(rows, rows, rows, grad, grad_t, bias, live)


def to_partner(packet, xor_value):
    groups = lax.axis_size("dp")

    def by(distance):
        route = [(group, group ^ distance) for group in range(groups)]
        return lambda block: lax.ppermute(block, "dp", route)

    return lax.switch(xor_value - 1, [by(distance) for distance in range(1, groups)], packet)


def on_device(
    queries, key_rows, value_rows_initial, grad_out, seg_ids, pair_mask, sender, moved_seq
):
    count_rows = grad_out.shape[0]
    shards = lax.axis_size("tensor")
    local = queries.shape[0]
    split = lambda block: block.reshape(local, shards, block.shape[1] // shards)
    outgoing = jnp.concatenate(
        [split(queries), split(key_rows), split(value_rows_initial)], axis=2
    ).transpose(1, 0, 2)
    width = outgoing.shape[2]
    query_width = grad_out.shape[1]
    rows = lax.all_to_all(outgoing, "tensor", split_axis=0, concat_axis=0, tiled=True)
    rows = rows.reshape(count_rows, width)

    group = lax.axis_index("dp")
    xor_value = pair_mask[0]
    partner = jnp.bitwise_xor(group, xor_value)
    own = seg_ids[group]
    theirs = seg_ids[partner]
    giving = sender[group] == 1
    moved_label = moved_seq[group]
    live = jnp.sum((own < SEQS).astype(jnp.int32))
    start = jnp.sum((own < moved_label).astype(jnp.int32))
    count = jnp.sum((theirs == moved_seq[partner]).astype(jnp.int32))
    positions = jnp.arange(count_rows, dtype=jnp.int32)
    slots = jnp.arange(MOVE, dtype=jnp.int32)
    is_live = own != SEQS
    is_moved = giving & (own == moved_label)
    keep = is_live & ~is_moved

    packet = to_partner(lax.dynamic_slice_in_dim(grad_out, live, MOVE, 0), xor_value)
    place = (is_moved[:, None] & (positions[:, None] - start == slots[None, :])).astype(
        jnp.bfloat16
    )
    grad = jnp.where(
        keep[:, None], grad_out, dot(place, packet, 1, 0).astype(jnp.bfloat16)
    )
    grad_t = grad.T
    allowed = (
        (own[:, None] == own[None, :])
        & is_live[None, :]
        & (positions[:, None] <= positions[None, :])
    ) | (positions[:, None] == positions[None, :])
    bias = jnp.where(allowed, jnp.float32(0), jnp.float32(BLOCKED))
    attention, grads = attend(
        rows, grad, grad_t, bias, is_live.astype(jnp.float32)[None, :], count_rows
    )
    restored = lax.all_to_all(
        grads.reshape(shards, local, width), "tensor", split_axis=0, concat_axis=0, tiled=True
    )
    returning = to_partner(dot(place, attention, 0, 0).astype(jnp.bfloat16), xor_value)
    arrive = (
        ~giving
        & (positions[:, None] - live == slots[None, :])
        & (slots[None, :] < count)
    ).astype(jnp.bfloat16)
    attention = jnp.where(
        keep[:, None], attention, dot(arrive, returning, 1, 0).astype(jnp.bfloat16)
    )
    restored = restored.transpose(1, 0, 2)
    head_width = width - query_width
    joined = lambda block: block.reshape(local, -1)
    return (
        attention,
        joined(restored[:, :, :query_width]),
        joined(restored[:, :, query_width : query_width + head_width // 2]),
        joined(restored[:, :, query_width + head_width // 2 :]),
    )


def solution(mesh):
    rows = P(("dp", "tensor"), None)
    heads = P("dp", "tensor")
    return jax.shard_map(
        on_device,
        mesh=mesh,
        in_specs=(rows, rows, rows, heads, P(), P(), P(), P()),
        out_specs=(heads, rows, rows, rows),
        check_vma=False,
    )
```

time: 357 us -> 138 us (0.39)
  the two profiles are of different devices: /device:TPU:1 before, /device:TPU:17 now
where the time goes in v1:
time: 138 us; the launch traced here: 137 us
  waiting for transfers between devices  48.1 us (35%)
  starting transfers between devices  47.5 us (34%)
  local copies, waits for them, and re-layouts  13.1 us (9%)
  Pallas kernels  11.5 us (8%)
  other arithmetic  9.66 us (7%)
  matrix products  3.65 us (3%)
  between operations  3.6 us (3%)
    ppermute x2, waiting for transfers between devices, by(): return lambda block: lax.ppermute(block, 'dp', route)  48.1 us
    ppermute x2, starting transfers between devices, by(): return lambda block: lax.ppermute(block, 'dp', route)  35.1 us
    pallas_call x1, Pallas kernels, attend(): pl.pallas_call(functools.partial(attention_kernel, heads, tile), grid=(he...  11.5 us
    all_to_all x1, starting transfers between devices, on_device(): lax.all_to_all(outgoing, 'tensor', split_axis=0, concat_axis=0, tiled=True)  7.63 us
    unnamed x30, local copies, waits for them, and re-layouts  6.16 us
    all_to_all x1, starting transfers between devices, on_device(): lax.all_to_all(grads.reshape(shards, local, width), 'tensor', split_axis=...  4.72 us
    dot_general x3, matrix products, dot(): lax.dot_general(a, b, (((contract_a,), (contract_b,)), ((), ())), preferr...  3.65 us
  transfers between devices with their start and end apart: 4, of which 2 were waited for; matrix products, arithmetic and copies ran while one was open for 12% of the time, Pallas kernels for 0%

profile of v1, /device:TPU:17, one launch (start us, length us, event | category | flops | bytes accessed | tf_op | source)
XLA Modules:
  0.0 137.4 jit_solution(12888972405267903829)
XLA Ops:
  0.7 1.4 copy.37
  2.1 1.2 maximum_bitcast_fusion
  3.3 7.6 %all-to-all-start = ((bf16[8,64,1280]{2,1,0:T(8,128)(2,1)}), bf16[8,64,1280]{2,1,0:T(8,128)(2,1)S(1)}, u32[]{:S(2)}, u32[]{:S(2)}) async-start(bf16[8,64,1280]{2,1,0:T(8,128)(2,1)} %maximum_bitcast_fusion), calls=%async_computation | async-start | bytes 2621440 | tf_op jit(solution)/shard_map/all_to_all | solution.py:133
  12.9 1.4 convert_reduce_fusion.1
  17.6 46.5 %conditional.2 = (bf16[128,1024]{1,0:T(8,128)(2,1)}) conditional(s32[]{:T(128)} %clamp.4, bf16[128,1024]{1,0:T(8,128)(2,1)S(1)} %constant_dynamic-slice_fusion, bf16[128,1024]{1,0:T(8,128)(2,1)S(1)} %constant_dynamic-slice_fusion, bf16[128,1024]{1,0:T(8,128)(2,1)S(1)} %constant_dynamic-slice_fusion, ...), branch_computations={%region_2.0_spmd, %region_3.0_spmd, %region_4.0_spmd, %region_5.0_... | conditional | bytes 1048624 | solution.py:118
  17.6 20.8 %collective-permute-start.42 = (bf16[128,1024]{1,0:T(8,128)(2,1)S(1)}, bf16[128,1024]{1,0:T(8,128)(2,1)}, u32[]{:S(2)}, u32[]{:S(2)}) collective-permute-start(bf16[128,1024]{1,0:T(8,128)(2,1)S(1)} %param.42), channel_id=1, source_target_pairs={{0,344},{8,336},{16,328},{24,320},{32,376},{40,368},{48,360},{56,3... | collective-permute-start | bytes 786440 | tf_op jit(solution)/shard_map/cond/branch_42_fun/ppermute | solution.py:116
  38.5 25.6 %collective-permute-done.42 = bf16[128,1024]{1,0:T(8,128)(2,1)} collective-permute-done((bf16[128,1024]{1,0:T(8,128)(2,1)S(1)}, bf16[128,1024]{1,0:T(8,128)(2,1)}, u32[]{:S(2)}, u32[]{:S(2)}) %collective-permute-start.42) | collective-permute-done | bytes 262176 | tf_op jit(solution)/shard_map/cond/branch_42_fun/ppermute | solution.py:116
  64.1 1.3 iota_subtract_fusion
  66.7 1.6 %fusion = bf16[512,1024]{0,1:T(8,128)(2,1)S(1)} fusion(bf16[512,1024]{0,1:T(8,128)(2,1)S(1)} %copy.16, bf16[128,1024]{1,0:T(8,128)(2,1)} %get-tuple-element.280, pred[512]{0:T(512)(128)(4,1)S(1)} %get-tuple-element.270, s32[512]{0:T(512)S(1)} %get-tuple-element.279, pred[512]{0:T(512)(128)(4,1)S(1)} %get-tuple-element.271), kind=kOutput, calls=%fused_computation.2 | convolution fusion | flops 135397376 | bytes 2362368 | tf_op jit(solution)/shard_map/dot_general | solution.py:19
  68.3 1.3 copy.17.g_ref
  69.6 1.2 fusion.4.bias_ref
  70.8 1.2 copy-done.2
  72.1 1.2 copy-done.3
  73.3 11.5 %attention.1 = (bf16[512,1024]{1,0:T(8,128)(2,1)S(1)}, bf16[512,1280]{1,0:T(8,128)(2,1)S(1)}) custom-call(bf16[512,1280]{1,0:T(8,128)(2,1)S(1)} %bitcast.43, bf16[512,1280]{1,0:T(8,128)(2,1)S(1)} %bitcast.44, bf16[512,1280]{1,0:T(8,128)(2,1)S(1)} %bitcast.45, bf16[512,1024]{1,0:T(8,128)(2,1)S(1)} %copy-done.2, bf16[1024,512]{1,0:T(8,128)(2,1)S(1)} %bitcast.42, ...), custom_call_target="tpu_custom_call" | custom-call | flops 3221225472 | bytes 8388608 | tf_op jit(solution)/shard_map/attention/pallas_call | solution.py:75
  84.8 1.1 copy-done.1
  85.9 4.7 %all-to-all-start.1 = ((bf16[8,64,1280]{2,1,0:T(8,128)(2,1)}), bf16[8,64,1280]{2,1,0:T(8,128)(2,1)S(1)}, u32[]{:S(2)}, u32[]{:S(2)}) async-start(bf16[8,64,1280]{2,1,0:T(8,128)(2,1)} %bitcast.46), calls=%async_computation.1 | async-start | bytes 2621440 | tf_op jit(solution)/shard_map/all_to_all | solution.py:169
  90.6 2.0 %fusion.18 = s32[]{:T(128)} fusion(s32[64,512]{1,0:T(8,128)} %param.138, s32[]{:T(128)S(6)} %select_n.27, s32[]{:T(128)} %bitcast.7), kind=kLoop, calls=%fused_computation.34 | loop fusion | flops 1535 | bytes 2060 | tf_op jit(solution)/shard_map/reduce_sum | solution.py:145
  92.6 1.2 iota_compare_fusion.4
  94.9 37.0 %conditional.3 = (bf16[128,1024]{1,0:T(8,128)(2,1)}) conditional(s32[]{:T(128)} %clamp.4, bf16[128,1024]{1,0:T(8,128)(2,1)S(1)} %convolution_convert_fusion.2, bf16[128,1024]{1,0:T(8,128)(2,1)S(1)} %convolution_convert_fusion.2, bf16[128,1024]{1,0:T(8,128)(2,1)S(1)} %convolution_convert_fusion.2, ...), branch_computations={%region_66.67_spmd, %region_67.68_spmd, %region_68.69_spmd, %regio... | conditional | bytes 1048624 | solution.py:118
  95.1 14.3 %collective-permute-start.105 = (bf16[128,1024]{1,0:T(8,128)(2,1)S(1)}, bf16[128,1024]{1,0:T(8,128)(2,1)}, u32[]{:S(2)}, u32[]{:S(2)}) collective-permute-start(bf16[128,1024]{1,0:T(8,128)(2,1)S(1)} %param.105), channel_id=1, source_target_pairs={{0,344},{8,336},{16,328},{24,320},{32,376},{40,368},{48,360},{56,3... | collective-permute-start | bytes 786440 | tf_op jit(solution)/shard_map/cond/branch_42_fun/ppermute | solution.py:116
  109.4 22.5 %collective-permute-done.105 = bf16[128,1024]{1,0:T(8,128)(2,1)} collective-permute-done((bf16[128,1024]{1,0:T(8,128)(2,1)S(1)}, bf16[128,1024]{1,0:T(8,128)(2,1)}, u32[]{:S(2)}, u32[]{:S(2)}) %collective-permute-start.105) | collective-permute-done | bytes 262176 | tf_op jit(solution)/shard_map/cond/branch_42_fun/ppermute | solution.py:116
  131.9 1.5 %fusion.1 = bf16[512,1024]{0,1:T(8,128)(2,1)S(1)} fusion(bf16[512,1024]{0,1:T(8,128)(2,1)S(1)} %copy.19, bf16[128,1024]{1,0:T(8,128)(2,1)} %get-tuple-element.281, pred[512]{0:T(512)(128)(4,1)S(1)} %copy-done.9, s32[512]{0:T(512)S(1)} %get-tuple-element.278, pred[128]{0:T(512)(128)(4,1)} %iota_compare_fusion.4, pred[]{:T(512)S(6)} %not.11), kind=kOutput, calls=%fused_computation.3 | convolution fusion | flops 135462912 | bytes 2361985 | tf_op jit(solution)/shard_map/dot_general | solution.py:19
  133.5 1.3 copy.23
  135.0 1.1 copy.29
  (39 shorter events, 6.5 us)
Async XLA Ops:
  0.6 1.4 %copy-start = (bf16[64,1024]{1,0:T(8,128)(2,1)S(1)}, bf16[64,1024]{1,0:T(8,128)(2,1)}, u32[]{:S(2)}) copy-start(bf16[64,1024]{1,0:T(8,128)(2,1)} %param.135) | copy-start | bytes 393220
  0.6 1.4 %copy-start.5 = (bf16[64,1024]{1,0:T(8,128)(2,1)S(1)}, bf16[64,1024]{1,0:T(8,128)(2,1)}, u32[]{:S(2)}) copy-start(bf16[64,1024]{1,0:T(8,128)(2,1)} %param.136) | copy-start | bytes 393220
  3.3 7.6 %copy-start.11 = (s32[64]{0:T(128)S(1)}, s32[64]{0:T(128)}, u32[]{:S(2)}) copy-start(s32[64]{0:T(128)} %param.139) | copy-start | bytes 772
  3.3 7.7 %copy-start.12 = (s32[64]{0:T(128)S(1)}, s32[64]{0:T(128)}, u32[]{:S(2)}) copy-start(s32[64]{0:T(128)} %param.140) | copy-start | bytes 772
  3.3 8.3 %copy-start.10 = (s32[64]{0:T(128)S(1)}, s32[64]{0:T(128)}, u32[]{:S(2)}) copy-start(s32[64]{0:T(128)} %param.141) | copy-start | bytes 772
  3.3 12.3 %copy-start.4 = (bf16[512,1024]{1,0:T(8,128)(2,1)S(1)}, bf16[512,1024]{1,0:T(8,128)(2,1)}, u32[]{:S(2)}) copy-start(bf16[512,1024]{1,0:T(8,128)(2,1)} %param.137) | copy-start | bytes 3145732
  3.3 67.5 %all-to-all-start = ((bf16[8,64,1280]{2,1,0:T(8,128)(2,1)}), bf16[8,64,1280]{2,1,0:T(8,128)(2,1)S(1)}, u32[]{:S(2)}, u32[]{:S(2)}) async-start(bf16[8,64,1280]{2,1,0:T(8,128)(2,1)} %maximum_bitcast_fusion), calls=%async_computation | async-start | bytes 2621440 | tf_op jit(solution)/shard_map/all_to_all | solution.py:133
  17.6 46.5 %collective-permute-start.42 = (bf16[128,1024]{1,0:T(8,128)(2,1)S(1)}, bf16[128,1024]{1,0:T(8,128)(2,1)}, u32[]{:S(2)}, u32[]{:S(2)}) collective-permute-start(bf16[128,1024]{1,0:T(8,128)(2,1)S(1)} %param.42), channel_id=1, source_target_pairs={{0,344},{8,336},{16,328},{24,320},{32,376},{40,368},{48,360},{56,3... | collective-permute-start | bytes 786440 | tf_op jit(solution)/shard_map/cond/branch_42_fun/ppermute | solution.py:116
  66.1 0.5 copy-start.6
  66.1 0.6 copy-start.8
  70.8 1.2 copy-start.2
  72.1 1.2 copy-start.3
  84.8 1.1 copy-start.1
  85.9 48.9 %all-to-all-start.1 = ((bf16[8,64,1280]{2,1,0:T(8,128)(2,1)}), bf16[8,64,1280]{2,1,0:T(8,128)(2,1)S(1)}, u32[]{:S(2)}, u32[]{:S(2)}) async-start(bf16[8,64,1280]{2,1,0:T(8,128)(2,1)} %bitcast.46), calls=%async_computation.1 | async-start | bytes 2621440 | tf_op jit(solution)/shard_map/all_to_all | solution.py:169
  90.6 3.7 %copy-start.7 = (pred[512]{0:T(512)(128)(4,1)S(1)}, pred[512]{0:T(512)(128)(4,1)}, u32[]{:S(2)}) copy-start(pred[512]{0:T(512)(128)(4,1)} %copy-done.6) | copy-start | bytes 1540
  93.8 38.2 %copy-start.9 = (pred[512]{0:T(512)(128)(4,1)S(1)}, pred[512]{0:T(512)(128)(4,1)}, u32[]{:S(2)}) copy-start(pred[512]{0:T(512)(128)(4,1)} %copy-done.8) | copy-start | bytes 1540
  95.1 36.8 %collective-permute-start.105 = (bf16[128,1024]{1,0:T(8,128)(2,1)S(1)}, bf16[128,1024]{1,0:T(8,128)(2,1)}, u32[]{:S(2)}, u32[]{:S(2)}) collective-permute-start(bf16[128,1024]{1,0:T(8,128)(2,1)S(1)} %param.105), channel_id=1, source_target_pairs={{0,344},{8,336},{16,328},{24,320},{32,376},{40,368},{48,360},{56,3... | collective-permute-start | bytes 786440 | tf_op jit(solution)/shard_map/cond/branch_42_fun/ppermute | solution.py:116

commit v2 on v1

v2 whole, which is shorter than its diff:
```python
import functools

import jax
import jax.numpy as jnp
from jax import lax
from jax.experimental import pallas as pl
from jax.experimental.pallas import tpu as pltpu
from jax.sharding import PartitionSpec as P

HEAD = 128
SEQS = 8
MOVE = 128
FACTOR = HEAD**-0.5
LOG2E = 1.4426950408889634
BLOCKED = -1e30
TILE = 128
TOGETHER = 4
F32 = jnp.float32
BF16 = jnp.bfloat16
VMEM = pl.BlockSpec(memory_space=pltpu.VMEM)
SMEM = pl.BlockSpec(memory_space=pltpu.SMEM)
HBM = pl.BlockSpec(memory_space=pltpu.HBM)


def dot(a, b, contract_a, contract_b):
    return lax.dot_general(
        a, b, (((contract_a,), (contract_b,)), ((), ())), preferred_element_type=F32
    )


def params(mebibytes):
    return pltpu.CompilerParams(vmem_limit_bytes=mebibytes * 2**20)


def cost(flops, moved):
    return pl.CostEstimate(flops=flops, bytes_accessed=moved, transcendentals=0)


def slots(parts, shards):
    first = 0
    for part in parts:
        width = part.shape[1] // shards
        yield part, width, first
        first += width


def pack_kernel(q_ref, k_ref, v_ref, packed_ref, block_ref, in_sems, out_sems):
    shards = packed_ref.shape[0]
    arriving = []
    for shard in range(shards):
        for index, (part, width, first) in enumerate(slots((q_ref, k_ref, v_ref), shards)):
            copy = pltpu.make_async_copy(
                part.at[:, shard * width : (shard + 1) * width],
                block_ref.at[shard, :, first : first + width],
                in_sems.at[shard, index],
            )
            copy.start()
            arriving.append(copy)
    leaving = []
    for shard in range(shards):
        for copy in arriving[3 * shard : 3 * shard + 3]:
            copy.wait()
        copy = pltpu.make_async_copy(
            block_ref.at[shard], packed_ref.at[shard], out_sems.at[shard]
        )
        copy.start()
        leaving.append(copy)
    for copy in leaving:
        copy.wait()


def pack(queries, key_rows, value_rows, shards):
    local = queries.shape[0]
    width = (queries.shape[1] + key_rows.shape[1] + value_rows.shape[1]) // shards
    return pl.pallas_call(
        pack_kernel,
        in_specs=[HBM] * 3,
        out_specs=HBM,
        out_shape=jax.ShapeDtypeStruct((shards, local, width), BF16),
        scratch_shapes=[
            pltpu.VMEM((shards, local, width), BF16),
            pltpu.SemaphoreType.DMA((shards, 3)),
            pltpu.SemaphoreType.DMA((shards,)),
        ],
        compiler_params=params(56),
        cost_estimate=cost(0, 4 * local * width * shards),
        name="pack_rows",
    )(queries, key_rows, value_rows)


def unpack_kernel(packed_ref, q_ref, k_ref, v_ref, sems):
    shards = packed_ref.shape[0]
    leaving = []
    for shard in range(shards):
        for index, (part, width, first) in enumerate(slots((q_ref, k_ref, v_ref), shards)):
            copy = pltpu.make_async_copy(
                packed_ref.at[shard, :, first : first + width],
                part.at[:, shard * width : (shard + 1) * width],
                sems.at[shard, index],
            )
            copy.start()
            leaving.append(copy)
    for copy in leaving:
        copy.wait()


def unpack(packed, query_width, head_width):
    shards, local, _ = packed.shape
    shape = lambda width: jax.ShapeDtypeStruct((local, shards * width), BF16)
    return pl.pallas_call(
        unpack_kernel,
        in_specs=[VMEM],
        out_specs=[HBM] * 3,
        out_shape=[shape(query_width), shape(head_width), shape(head_width)],
        scratch_shapes=[pltpu.SemaphoreType.DMA((shards, 3))],
        compiler_params=params(8),
        cost_estimate=cost(0, 4 * packed.size),
        name="unpack_rows",
    )(packed)


def one_hot(hits):
    return hits.astype(F32).astype(BF16)


def iota(shape, dimension):
    return lax.broadcasted_iota(jnp.int32, shape, dimension)


def layout_kernel(
    group_ref, mask_ref, sender_ref, moved_ref, seg_ref, grad_ref, packet_ref, facts_ref, live_ref
):
    count = seg_ref.shape[1]
    group = group_ref[0]
    partner = jnp.bitwise_xor(group, mask_ref[0])
    giving = sender_ref[group] == 1
    own = seg_ref[pl.ds(group, 1), :]
    theirs = seg_ref[pl.ds(partner, 1), :]
    moved = jnp.where(giving, moved_ref[group], -1)
    number = lambda hits: jnp.sum(hits.astype(F32), axis=1, keepdims=True).astype(jnp.int32)
    live = number(own < SEQS)
    start = number(own < moved)
    handed = jnp.where(giving, 0, number(theirs == moved_ref[partner]))
    wide = lambda value: jnp.broadcast_to(value, (1, count))
    facts_ref[0:1, :] = own
    facts_ref[1:2, :] = jnp.full((1, count), moved, jnp.int32)
    facts_ref[2:3, :] = wide(start)
    facts_ref[3:4, :] = wide(live)
    facts_ref[4:5, :] = wide(handed)
    facts_ref[5:8, :] = jnp.zeros((3, count), jnp.int32)
    live_ref[0] = jnp.sum((own < SEQS).astype(F32)).astype(jnp.int32)
    take = one_hot(iota((MOVE, count), 1) - live == iota((MOVE, count), 0))
    packet_ref[...] = dot(take, grad_ref[...], 1, 0).astype(BF16)


def layout(group, pair_mask, sender, moved_seq, seg_ids, grad_out):
    count, width = grad_out.shape
    return pl.pallas_call(
        layout_kernel,
        in_specs=[SMEM] * 4 + [VMEM] * 2,
        out_specs=[VMEM, VMEM, SMEM],
        out_shape=[
            jax.ShapeDtypeStruct((MOVE, width), BF16),
            jax.ShapeDtypeStruct((8, count), jnp.int32),
            jax.ShapeDtypeStruct((1,), jnp.int32),
        ],
        compiler_params=params(8),
        cost_estimate=cost(2 * MOVE * count * width, 2**20),
        name="layout",
    )(group, pair_mask, sender, moved_seq, seg_ids, grad_out)


def finish_kernel(live_ref, facts_ref, packet_ref, out_ref, final_ref, window_ref, sem):
    del out_ref
    count = final_ref.shape[0]
    size = window_ref.shape[0]
    base = pl.multiple_of(jnp.minimum(live_ref[0] // 16 * 16, count - size), 16)
    rows = final_ref.at[pl.ds(base, size), :]
    fetch = pltpu.make_async_copy(rows, window_ref, sem.at[0])
    fetch.start()
    fetch.wait()
    row = iota((size, MOVE), 0) + base
    slot = iota((size, MOVE), 1)
    arrive = one_hot((row - facts_ref[3:4, :MOVE] == slot) & (slot < facts_ref[4:5, :MOVE]))
    window_ref[...] += dot(arrive, packet_ref[...], 1, 0).astype(BF16)
    store = pltpu.make_async_copy(window_ref, rows, sem.at[1])
    store.start()
    store.wait()


def finish(live, facts, packet, attention):
    return pl.pallas_call(
        finish_kernel,
        in_specs=[SMEM, VMEM, VMEM, HBM],
        out_specs=HBM,
        out_shape=jax.ShapeDtypeStruct(attention.shape, BF16),
        scratch_shapes=[
            pltpu.VMEM((MOVE + 16, attention.shape[1]), BF16),
            pltpu.SemaphoreType.DMA((2,)),
        ],
        input_output_aliases={3: 0},
        compiler_params=params(8),
        cost_estimate=cost(2 * MOVE * MOVE * attention.shape[1], 2**20),
        name="finish_out",
    )(live, facts, packet, attention)


def attention_kernel(
    x_ref, facts_ref, packet_hbm, grad_hbm,
    final_hbm, returning_ref, grads_hbm,
    packet_ref, g_ref, gt_ref, bias_ref, keep_ref, place_ref,
    kt_ref, vt_ref, dk_ref, dv_ref, o_ref, out_ref, in_sems, out_sems,
):
    count, width = x_ref.shape
    heads = width // HEAD - 2
    steps = heads // TOGETHER
    block = lambda step: slice(step * TOGETHER * HEAD, (step + 1) * TOGETHER * HEAD)
    fetches = [pltpu.make_async_copy(packet_hbm, packet_ref, in_sems.at[steps])] + [
        pltpu.make_async_copy(
            grad_hbm.at[:, block(step)], g_ref.at[:, block(step)], in_sems.at[step]
        )
        for step in range(steps)
    ]
    for fetch in fetches:
        fetch.start()

    own = facts_ref[0:1, :]
    moved, start = facts_ref[1:2, :MOVE], facts_ref[2:3, :MOVE]
    live = (own < SEQS).astype(F32)
    own_column = jnp.broadcast_to(own.astype(F32), (MOVE, count)).T.astype(jnp.int32)
    row, slot = iota((count, MOVE), 0), iota((count, MOVE), 1)
    keep_ref[...] = one_hot((own_column < SEQS) & (own_column != moved))
    place_ref[...] = one_hot((own_column == moved) & (row - start == slot))
    place_t = one_hot(
        (own == facts_ref[1:2, :]) & (iota((MOVE, count), 1) - facts_ref[2:3, :] == iota((MOVE, count), 0))
    )
    for first in range(0, count, MOVE):
        columns = slice(first, first + MOVE)
        seen = first + MOVE
        u, t = row[:seen], slot[:seen] + first
        theirs = own_column[:seen]
        allowed = ((theirs == own[:, columns]) & (theirs < SEQS) & (u <= t)) | (u == t)
        bias_ref[:seen, columns] = jnp.where(allowed, F32(0), F32(BLOCKED))
    k_ref = x_ref.at[:, heads * HEAD : (heads + 1) * HEAD]
    v_ref = x_ref.at[:, (heads + 1) * HEAD :]
    kt_ref[...] = k_ref[...].T
    vt_ref[...] = v_ref[...].T
    dk_ref[...] = jnp.zeros_like(dk_ref)
    dv_ref[...] = jnp.zeros_like(dv_ref)

    def send(source, target, columns, index):
        return pltpu.make_async_copy(
            source.at[:, columns], target.at[:, columns], out_sems.at[index]
        )

    leaving = []
    for step in range(steps):
        columns = block(step)
        here = [
            slice(head * HEAD, (head + 1) * HEAD)
            for head in range(step * TOGETHER, (step + 1) * TOGETHER)
        ]
        work = [
            (head, slice(first, first + TILE), first + TILE)
            for first in range(0, count, TILE)
            for head in here
        ]
        scores, grad_probs, probs, outs = [], [], [], []
        for head, rows, seen in work:
            scores.append(dot(k_ref[:seen, :], x_ref[rows, head], 1, 1) + bias_ref[:seen, rows])
        if step == 0:
            fetches[0].wait()
        fetches[1 + step].wait()
        for head in here:
            placed = dot(place_ref[...], packet_ref[:, head], 1, 0).astype(BF16)
            merged = g_ref[:, head] * keep_ref[...] + placed
            g_ref[:, head] = merged
            gt_ref[head, :] = merged.T
        for head, rows, seen in work:
            grad_probs.append(dot(v_ref[:seen, :], gt_ref[head, rows], 1, 0))
        for (head, rows, seen), score in zip(work, scores):
            peak = jnp.max(score, axis=0, keepdims=True)
            weights = jnp.exp2((score - peak) * (FACTOR * LOG2E))
            prob = weights * (1.0 / jnp.sum(weights, axis=0, keepdims=True))
            low = prob.astype(BF16)
            out = dot(vt_ref[:, :seen], low, 1, 0)
            out = (out * live[:, rows]).astype(BF16)
            o_ref[rows, head] = out.T
            dv_ref[:seen, :] += dot(low, g_ref[rows, head], 1, 0)
            probs.append(prob)
            outs.append(out)
        for (head, rows, seen), prob, grad_prob, out in zip(work, probs, grad_probs, outs):
            center = jnp.sum(
                gt_ref[head, rows].astype(F32) * out.astype(F32), axis=0, keepdims=True
            )
            grad_score = (prob * (grad_prob - center)).astype(BF16)
            grad_q = dot(kt_ref[:, :seen], grad_score, 1, 0) * FACTOR
            out_ref[rows, head] = grad_q.astype(BF16).T
            dk_ref[:seen, :] += dot(grad_score, x_ref[rows, head], 1, 0)
        leaving.append(send(out_ref, grads_hbm, columns, 2 * step))
        leaving[-1].start()
        returning_ref[:, columns] = dot(place_t, o_ref[:, columns], 1, 0).astype(BF16)
        for head in here:
            o_ref[:, head] = o_ref[:, head] * keep_ref[...]
        leaving.append(send(o_ref, final_hbm, columns, 2 * step + 1))
        leaving[-1].start()
    out_ref[:, heads * HEAD : (heads + 1) * HEAD] = (dk_ref[...] * FACTOR).astype(BF16)
    out_ref[:, (heads + 1) * HEAD :] = dv_ref[...].astype(BF16)
    leaving.append(send(out_ref, grads_hbm, slice(heads * HEAD, width), 2 * steps))
    leaving[-1].start()
    for copy in leaving:
        copy.wait()


def attend(rows, facts, packet, grad):
    count, width = rows.shape
    heads = width // HEAD - 2
    steps = heads // TOGETHER
    return pl.pallas_call(
        attention_kernel,
        in_specs=[VMEM, VMEM, HBM, HBM],
        out_specs=[HBM, VMEM, HBM],
        out_shape=[
            jax.ShapeDtypeStruct((count, heads * HEAD), BF16),
            jax.ShapeDtypeStruct((MOVE, heads * HEAD), BF16),
            jax.ShapeDtypeStruct((count, width), BF16),
        ],
        scratch_shapes=[
            pltpu.VMEM((MOVE, heads * HEAD), BF16),
            pltpu.VMEM((count, heads * HEAD), BF16),
            pltpu.VMEM((heads * HEAD, count), BF16),
            pltpu.VMEM((count, count), F32),
            pltpu.VMEM((count, MOVE), BF16),
            pltpu.VMEM((count, MOVE), BF16),
            pltpu.VMEM((HEAD, count), BF16),
            pltpu.VMEM((HEAD, count), BF16),
            pltpu.VMEM((count, HEAD), F32),
            pltpu.VMEM((count, HEAD), F32),
            pltpu.VMEM((count, heads * HEAD), BF16),
            pltpu.VMEM((count, width), BF16),
            pltpu.SemaphoreType.DMA((steps + 1,)),
            pltpu.SemaphoreType.DMA((2 * steps + 1,)),
        ],
        compiler_params=params(48),
        cost_estimate=cost(12 * heads * count * count * HEAD, 8 * 2**20),
        name="attention",
    )(rows, facts, packet, grad)


def to_partner(packet, xor_value):
    groups = lax.axis_size("dp")

    def by(distance):
        route = [(group, group ^ distance) for group in range(groups)]
        return lambda block: lax.ppermute(block, "dp", route)

    return lax.switch(xor_value - 1, [by(distance) for distance in range(1, groups)], packet)


def on_device(
    queries, key_rows, value_rows_initial, grad_out, seg_ids, pair_mask, sender, moved_seq
):
    count, query_width = grad_out.shape
    shards = lax.axis_size("tensor")
    outgoing = pack(queries, key_rows, value_rows_initial, shards)
    rows = lax.all_to_all(outgoing, "tensor", split_axis=0, concat_axis=0, tiled=True)
    width = rows.shape[2]

    group = lax.axis_index("dp").reshape(1)
    packet, facts, live = layout(group, pair_mask, sender, moved_seq, seg_ids, grad_out)
    packet = to_partner(packet, pair_mask[0])
    attention, returning, grads = attend(rows.reshape(count, width), facts, packet, grad_out)
    restored = lax.all_to_all(
        grads.reshape(outgoing.shape), "tensor", split_axis=0, concat_axis=0, tiled=True
    )
    returning = to_partner(returning, pair_mask[0])
    attention = finish(live, facts, returning, attention)
    return (attention, *unpack(restored, query_width, (width - query_width) // 2))


def solution(mesh):
    rows = P(("dp", "tensor"), None)
    heads = P("dp", "tensor")
    return jax.shard_map(
        on_device,
        mesh=mesh,
        in_specs=(rows, rows, rows, heads, P(), P(), P(), P()),
        out_specs=(heads, rows, rows, rows),
        check_vma=False,
    )
```

time: 138 us -> 106 us (0.77)
  the two profiles are of different devices: /device:TPU:17 before, /device:TPU:1 now
where the time goes in v2:
time: 106 us; the launch traced here: 104 us
  starting transfers between devices  49.6 us (47%)
  waiting for transfers between devices  37.2 us (35%)
  Pallas kernels  16.2 us (15%)
    ppermute x2, waiting for transfers between devices, by(): return lambda block: lax.ppermute(block, 'dp', route)  37.2 us
    ppermute x2, starting transfers between devices, by(): return lambda block: lax.ppermute(block, 'dp', route)  30.2 us
    all_to_all x1, starting transfers between devices, on_device(): lax.all_to_all(outgoing, 'tensor', split_axis=0, concat_axis=0, tiled=True)  10.3 us
    all_to_all x1, starting transfers between devices, on_device(): lax.all_to_all(grads.reshape(outgoing.shape), 'tensor', split_axis=0, con...  9.08 us
    pallas_call x1, Pallas kernels, attend(): pl.pallas_call(attention_kernel, in_specs=[VMEM, VMEM, HBM, HBM], out_spe...  7.89 us
    pallas_call x1, Pallas kernels, finish(): pl.pallas_call(finish_kernel, in_specs=[SMEM, VMEM, VMEM, HBM], out_specs...  3.51 us
    pallas_call x1, Pallas kernels, pack(): pl.pallas_call(pack_kernel, in_specs=[HBM] * 3, out_specs=HBM, out_shape=...  2.39 us
  transfers between devices with their start and end apart: 4, of which 2 were waited for; matrix products, arithmetic and copies ran while one was open for 0% of the time, Pallas kernels for 5%

profile of v2, /device:TPU:1, one launch (start us, length us, event | category | flops | bytes accessed | tf_op | source)
XLA Modules:
  0.0 104.0 jit_solution(13857863372621859950)
XLA Ops:
  0.6 2.4 %pack_rows.1 = bf16[8,64,1280]{2,1,0:T(8,128)(2,1)} custom-call(bf16[64,8192]{1,0:T(8,128)(2,1)} %q_ref.1, bf16[64,1024]{1,0:T(8,128)(2,1)} %k_ref.1, bf16[64,1024]{1,0:T(8,128)(2,1)} %v_ref.1), custom_call_target="tpu_custom_call" | custom-call | bytes 2621440 | tf_op jit(solution)/shard_map/pack_rows/pallas_call | solution.py:75
  3.0 0.0 copy-start.2
  3.0 0.0 copy-start
  3.1 0.0 copy-start.1
  3.1 0.0 copy-start.3
  3.1 0.0 copy-start.4
  3.1 10.3 %all-to-all-start = ((bf16[8,64,1280]{2,1,0:T(8,128)(2,1)}), bf16[8,64,1280]{2,1,0:T(8,128)(2,1)S(1)}, u32[]{:S(2)}, u32[]{:S(2)}) async-start(bf16[8,64,1280]{2,1,0:T(8,128)(2,1)} %pack_rows.1), calls=%async_computation | async-start | bytes 2621440 | tf_op jit(solution)/shard_map/all_to_all | solution.py:366
  13.3 0.0 copy-done.2
  13.4 0.0 copy-done
  13.4 0.0 copy-done.1
  13.4 0.0 copy-done.3
  13.4 1.2 %layout.1 = (bf16[128,1024]{1,0:T(8,128)(2,1)S(1)}, s32[8,512]{1,0:T(8,128)S(1)}, s32[1]{0:T(128)}) custom-call(s32[1]{0:T(128)} %bitcast.group_ref, s32[64]{0:T(128)S(1)} %copy-done.2, s32[64]{0:T(128)S(1)} %copy-done.3, s32[64]{0:T(128)S(1)} %copy-done.4, s32[64,512]{1,0:T(8,128)S(1)} %copy-done.1, bf16[512,1024]{1,0:T(8,128)(2,1)S(1)} %copy-done), custom_call_target="tpu_custom_call" | custom-call | flops 134217728 | bytes 1048576 | tf_op jit(solution)/shard_map/layout/pallas_call | solution.py:158
  14.6 37.6 %conditional.2 = (bf16[128,1024]{1,0:T(8,128)(2,1)}) conditional(s32[]{:T(128)} %bitcast.1, bf16[128,1024]{1,0:T(8,128)(2,1)S(1)} %get-tuple-element.269, bf16[128,1024]{1,0:T(8,128)(2,1)S(1)} %get-tuple-element.269, bf16[128,1024]{1,0:T(8,128)(2,1)S(1)} %get-tuple-element.269, ...), branch_computations={%region_0.0_spmd, %region_1.0_spmd, %region_2.0_spmd, %region_3.0_... | conditional | bytes 1048624 | solution.py:357
  14.7 19.0 %collective-permute-start.56 = (bf16[128,1024]{1,0:T(8,128)(2,1)S(1)}, bf16[128,1024]{1,0:T(8,128)(2,1)}, u32[]{:S(2)}, u32[]{:S(2)}) collective-permute-start(bf16[128,1024]{1,0:T(8,128)(2,1)S(1)} %param.56), channel_id=1, source_target_pairs={{0,456},{8,448},{16,472},{24,464},{32,488},{40,480},{48,504},{56,4... | collective-permute-start | bytes 786440 | tf_op jit(solution)/shard_map/cond/branch_56_fun/ppermute | solution.py:355
  33.7 18.5 %collective-permute-done.56 = bf16[128,1024]{1,0:T(8,128)(2,1)} collective-permute-done((bf16[128,1024]{1,0:T(8,128)(2,1)S(1)}, bf16[128,1024]{1,0:T(8,128)(2,1)}, u32[]{:S(2)}, u32[]{:S(2)}) %collective-permute-start.56) | collective-permute-done | bytes 262176 | tf_op jit(solution)/shard_map/cond/branch_56_fun/ppermute | solution.py:355
  52.2 0.0 all-to-all-done
  52.2 7.9 %attention.1 = (bf16[512,1024]{1,0:T(8,128)(2,1)}, bf16[128,1024]{1,0:T(8,128)(2,1)S(1)}, bf16[512,1280]{1,0:T(8,128)(2,1)}) custom-call(bf16[512,1280]{1,0:T(8,128)(2,1)S(1)} %bitcast.5, s32[8,512]{1,0:T(8,128)S(1)} %get-tuple-element.268.facts_ref, bf16[128,1024]{1,0:T(8,128)(2,1)} %get-tuple-element.276.packet_hbm, bf16[512,1024]{1,0:T(8,128)(2,1)S(1)} %copy-done), custom_call_target="tpu_custom_call" | custom-call | flops 3221225472 | bytes 8388608 | tf_op jit(solution)/shard_map/attention/pallas_call | solution.py:319
  60.1 9.1 %all-to-all-start.1 = ((bf16[8,64,1280]{2,1,0:T(8,128)(2,1)}), bf16[8,64,1280]{2,1,0:T(8,128)(2,1)S(1)}, u32[]{:S(2)}, u32[]{:S(2)}) async-start(bf16[8,64,1280]{2,1,0:T(8,128)(2,1)} %bitcast.3), calls=%async_computation.1 | async-start | bytes 2621440 | tf_op jit(solution)/shard_map/all_to_all | solution.py:373
  69.2 29.9 %conditional.3 = (bf16[128,1024]{1,0:T(8,128)(2,1)}) conditional(s32[]{:T(128)} %bitcast.1, bf16[128,1024]{1,0:T(8,128)(2,1)S(1)} %get-tuple-element.270, bf16[128,1024]{1,0:T(8,128)(2,1)S(1)} %get-tuple-element.270, bf16[128,1024]{1,0:T(8,128)(2,1)S(1)} %get-tuple-element.270, ...), branch_computations={%region_63.0_spmd, %region_64.0_spmd, %region_65.0_spmd, %region_6... | conditional | bytes 1048624 | solution.py:357
  69.2 11.2 %collective-permute-start.119 = (bf16[128,1024]{1,0:T(8,128)(2,1)S(1)}, bf16[128,1024]{1,0:T(8,128)(2,1)}, u32[]{:S(2)}, u32[]{:S(2)}) collective-permute-start(bf16[128,1024]{1,0:T(8,128)(2,1)S(1)} %param.119), channel_id=1, source_target_pairs={{0,456},{8,448},{16,472},{24,464},{32,488},{40,480},{48,504},{56,4... | collective-permute-start | bytes 786440 | tf_op jit(solution)/shard_map/cond/branch_56_fun/ppermute | solution.py:355
  80.4 18.7 %collective-permute-done.119 = bf16[128,1024]{1,0:T(8,128)(2,1)} collective-permute-done((bf16[128,1024]{1,0:T(8,128)(2,1)S(1)}, bf16[128,1024]{1,0:T(8,128)(2,1)}, u32[]{:S(2)}, u32[]{:S(2)}) %collective-permute-start.119) | collective-permute-done | bytes 262176 | tf_op jit(solution)/shard_map/cond/branch_56_fun/ppermute | solution.py:355
  99.1 3.5 %finish_out.1 = bf16[512,1024]{1,0:T(8,128)(2,1)} custom-call(s32[1]{0:T(128)} %get-tuple-element.267.live_ref, s32[8,512]{1,0:T(8,128)S(1)} %get-tuple-element.268.facts_ref, bf16[128,1024]{1,0:T(8,128)(2,1)} %get-tuple-element.277.packet_ref, bf16[512,1024]{1,0:T(8,128)(2,1)} %get-tuple-element.271.out_ref), custom_call_target="tpu_custom_call", output_to_operand_aliasing={{}: (3, {})} | custom-call | flops 33554432 | bytes 1048576 | tf_op jit(solution)/shard_map/finish_out/pallas_call | solution.py:192
  102.6 0.0 all-to-all-done.1.packed_ref
  102.6 1.2 %unpack_rows.1 = (bf16[64,8192]{1,0:T(8,128)(2,1)}, bf16[64,1024]{1,0:T(8,128)(2,1)}, bf16[64,1024]{1,0:T(8,128)(2,1)}) custom-call(bf16[8,64,1280]{2,1,0:T(8,128)(2,1)S(1)} %all-to-all-done.1.packed_ref), custom_call_target="tpu_custom_call" | custom-call | bytes 2621440 | tf_op jit(solution)/shard_map/unpack_rows/pallas_call | solution.py:110
  (1 shorter events, 0.0 us)
Async XLA Ops:
  3.0 10.3 %copy-start.2 = (s32[64]{0:T(128)S(1)}, s32[64]{0:T(128)}, u32[]{:S(2)}) copy-start(s32[64]{0:T(128)} %mask_ref.1) | copy-start | bytes 772
  3.0 10.4 %copy-start = (bf16[512,1024]{1,0:T(8,128)(2,1)S(1)}, bf16[512,1024]{1,0:T(8,128)(2,1)}, u32[]{:S(2)}) copy-start(bf16[512,1024]{1,0:T(8,128)(2,1)} %grad_hbm.1) | copy-start | bytes 3145732
  3.1 10.3 %copy-start.1 = (s32[64,512]{1,0:T(8,128)S(1)}, s32[64,512]{1,0:T(8,128)}, u32[]{:S(2)}) copy-start(s32[64,512]{1,0:T(8,128)} %seg_ref.1) | copy-start | bytes 393220
  3.1 10.3 %copy-start.3 = (s32[64]{0:T(128)S(1)}, s32[64]{0:T(128)}, u32[]{:S(2)}) copy-start(s32[64]{0:T(128)} %sender_ref.1) | copy-start | bytes 772
  3.1 10.3 %copy-start.4 = (s32[64]{0:T(128)S(1)}, s32[64]{0:T(128)}, u32[]{:S(2)}) copy-start(s32[64]{0:T(128)} %moved_ref.1) | copy-start | bytes 772
  3.1 49.1 %all-to-all-start = ((bf16[8,64,1280]{2,1,0:T(8,128)(2,1)}), bf16[8,64,1280]{2,1,0:T(8,128)(2,1)S(1)}, u32[]{:S(2)}, u32[]{:S(2)}) async-start(bf16[8,64,1280]{2,1,0:T(8,128)(2,1)} %pack_rows.1), calls=%async_computation | async-start | bytes 2621440 | tf_op jit(solution)/shard_map/all_to_all | solution.py:366
  14.7 37.5 %collective-permute-start.56 = (bf16[128,1024]{1,0:T(8,128)(2,1)S(1)}, bf16[128,1024]{1,0:T(8,128)(2,1)}, u32[]{:S(2)}, u32[]{:S(2)}) collective-permute-start(bf16[128,1024]{1,0:T(8,128)(2,1)S(1)} %param.56), channel_id=1, source_target_pairs={{0,456},{8,448},{16,472},{24,464},{32,488},{40,480},{48,504},{56,4... | collective-permute-start | bytes 786440 | tf_op jit(solution)/shard_map/cond/branch_56_fun/ppermute | solution.py:355
  60.1 42.5 %all-to-all-start.1 = ((bf16[8,64,1280]{2,1,0:T(8,128)(2,1)}), bf16[8,64,1280]{2,1,0:T(8,128)(2,1)S(1)}, u32[]{:S(2)}, u32[]{:S(2)}) async-start(bf16[8,64,1280]{2,1,0:T(8,128)(2,1)} %bitcast.3), calls=%async_computation.1 | async-start | bytes 2621440 | tf_op jit(solution)/shard_map/all_to_all | solution.py:373
  69.2 29.9 %collective-permute-start.119 = (bf16[128,1024]{1,0:T(8,128)(2,1)S(1)}, bf16[128,1024]{1,0:T(8,128)(2,1)}, u32[]{:S(2)}, u32[]{:S(2)}) collective-permute-start(bf16[128,1024]{1,0:T(8,128)(2,1)S(1)} %param.119), channel_id=1, source_target_pairs={{0,456},{8,448},{16,472},{24,464},{32,488},{40,480},{48,504},{56,4... | collective-permute-start | bytes 786440 | tf_op jit(solution)/shard_map/cond/branch_56_fun/ppermute | solution.py:355

commit v3 on v2

--- a/solution.py
+++ b/solution.py
@@ -172,17 +172,21 @@
 
 def finish_kernel(live_ref, facts_ref, packet_ref, out_ref, final_ref, window_ref, sem):
     del out_ref
-    count = final_ref.shape[0]
     size = window_ref.shape[0]
-    base = pl.multiple_of(jnp.minimum(live_ref[0] // 16 * 16, count - size), 16)
+    base = pl.multiple_of(
+        jnp.minimum(live_ref[0] // 16 * 16, final_ref.shape[0] - size), 16
+    )
     rows = final_ref.at[pl.ds(base, size), :]
     fetch = pltpu.make_async_copy(rows, window_ref, sem.at[0])
     fetch.start()
+    slot = iota((size, MOVE), 1)
+    arrive = one_hot(
+        (iota((size, MOVE), 0) + base - facts_ref[3:4, :MOVE] == slot)
+        & (slot < facts_ref[4:5, :MOVE])
+    )
+    placed = dot(arrive, packet_ref[...], 1, 0).astype(BF16)
     fetch.wait()
-    row = iota((size, MOVE), 0) + base
-    slot = iota((size, MOVE), 1)
-    arrive = one_hot((row - facts_ref[3:4, :MOVE] == slot) & (slot < facts_ref[4:5, :MOVE]))
-    window_ref[...] += dot(arrive, packet_ref[...], 1, 0).astype(BF16)
+    window_ref[...] += placed
     store = pltpu.make_async_copy(window_ref, rows, sem.at[1])
     store.start()
     store.wait()
@@ -253,6 +257,7 @@
             source.at[:, columns], target.at[:, columns], out_sems.at[index]
         )
 
+    everything = [slice(head * HEAD, (head + 1) * HEAD) for head in range(heads)]
     leaving = []
     for step in range(steps):
         columns = block(step)
@@ -260,43 +265,46 @@
             slice(head * HEAD, (head + 1) * HEAD)
             for head in range(step * TOGETHER, (step + 1) * TOGETHER)
         ]
-        work = [
-            (head, slice(first, first + TILE), first + TILE)
-            for first in range(0, count, TILE)
-            for head in here
-        ]
-        scores, grad_probs, probs, outs = [], [], [], []
-        for head, rows, seen in work:
-            scores.append(dot(k_ref[:seen, :], x_ref[rows, head], 1, 1) + bias_ref[:seen, rows])
+        tiles = [(slice(first, first + TILE), first + TILE) for first in range(0, count, TILE)]
+        queries, scores, grad_probs, probs, outs = [], [], [], [], []
+        for rows, seen in tiles:
+            queries.append(jnp.concatenate([x_ref[rows, head] for head in here], axis=0))
+            bias = jnp.concatenate([bias_ref[:seen, rows]] * TOGETHER, axis=1)
+            scores.append(dot(k_ref[:seen, :], queries[-1], 1, 1) + bias)
         if step == 0:
-            fetches[0].wait()
-        fetches[1 + step].wait()
-        for head in here:
+            for fetch in fetches:
+                fetch.wait()
+        for head in everything if step == 0 else ():
             placed = dot(place_ref[...], packet_ref[:, head], 1, 0).astype(BF16)
             merged = g_ref[:, head] * keep_ref[...] + placed
             g_ref[:, head] = merged
             gt_ref[head, :] = merged.T
-        for head, rows, seen in work:
-            grad_probs.append(dot(v_ref[:seen, :], gt_ref[head, rows], 1, 0))
-        for (head, rows, seen), score in zip(work, scores):
+        for rows, seen in tiles:
+            grad_t = jnp.concatenate([gt_ref[head, rows] for head in here], axis=1)
+            grad_probs.append(dot(v_ref[:seen, :], grad_t, 1, 0))
+        for (rows, seen), score in zip(tiles, scores):
             peak = jnp.max(score, axis=0, keepdims=True)
             weights = jnp.exp2((score - peak) * (FACTOR * LOG2E))
             prob = weights * (1.0 / jnp.sum(weights, axis=0, keepdims=True))
             low = prob.astype(BF16)
             out = dot(vt_ref[:, :seen], low, 1, 0)
-            out = (out * live[:, rows]).astype(BF16)
-            o_ref[rows, head] = out.T
-            dv_ref[:seen, :] += dot(low, g_ref[rows, head], 1, 0)
+            out = (out * jnp.concatenate([live[:, rows]] * TOGETHER, axis=1)).astype(BF16)
+            for index, head in enumerate(here):
+                o_ref[rows, head] = out[:, index * TILE : (index + 1) * TILE].T
+            grad = jnp.concatenate([g_ref[rows, head] for head in here], axis=0)
+            dv_ref[:seen, :] += dot(low, grad, 1, 0)
             probs.append(prob)
             outs.append(out)
-        for (head, rows, seen), prob, grad_prob, out in zip(work, probs, grad_probs, outs):
-            center = jnp.sum(
-                gt_ref[head, rows].astype(F32) * out.astype(F32), axis=0, keepdims=True
-            )
+        for (rows, seen), query, prob, grad_prob, out in zip(
+            tiles, queries, probs, grad_probs, outs
+        ):
+            grad_t = jnp.concatenate([gt_ref[head, rows] for head in here], axis=1)
+            center = jnp.sum(grad_t.astype(F32) * out.astype(F32), axis=0, keepdims=True)
             grad_score = (prob * (grad_prob - center)).astype(BF16)
-            grad_q = dot(kt_ref[:, :seen], grad_score, 1, 0) * FACTOR
-            out_ref[rows, head] = grad_q.astype(BF16).T
-            dk_ref[:seen, :] += dot(grad_score, x_ref[rows, head], 1, 0)
+            grad_q = (dot(kt_ref[:, :seen], grad_score, 1, 0) * FACTOR).astype(BF16)
+            for index, head in enumerate(here):
+                out_ref[rows, head] = grad_q[:, index * TILE : (index + 1) * TILE].T
+            dk_ref[:seen, :] += dot(grad_score, query, 1, 0)
         leaving.append(send(out_ref, grads_hbm, columns, 2 * step))
         leaving[-1].start()
         returning_ref[:, columns] = dot(place_t, o_ref[:, columns], 1, 0).astype(BF16)

time: 106 us -> 117 us (1.10); the launches traced: 104 us -> 116 us
  waiting for transfers between devices: 37.2 us -> 69.8 us
  starting transfers between devices: 49.6 us -> 30.1 us
    ppermute x2, waiting for transfers between devices: 37.2 us -> 69.8 us  [by(): return lambda block: lax.ppermute(block, 'dp', route)]
    ppermute x2, starting transfers between devices: 30.2 us -> 10.5 us  [by(): return lambda block: lax.ppermute(block, 'dp', route)]
  transfers between devices with their start and end apart: 4 -> 4, of which waited for: 2 -> 2; matrix products, arithmetic and copies ran while one was open for 0% -> 0% of each run, Pallas kernels for 5% -> 4%
where the time goes in v3:
time: 117 us; the launch traced here: 116 us
  waiting for transfers between devices  69.8 us (60%)
  starting transfers between devices  30.1 us (26%)
  Pallas kernels  15.5 us (13%)
    ppermute x2, waiting for transfers between devices, by(): return lambda block: lax.ppermute(block, 'dp', route)  69.8 us
    ppermute x2, starting transfers between devices, by(): return lambda block: lax.ppermute(block, 'dp', route)  10.5 us
    all_to_all x1, starting transfers between devices, on_device(): lax.all_to_all(outgoing, 'tensor', split_axis=0, concat_axis=0, tiled=True)  10.3 us
    all_to_all x1, starting transfers between devices, on_device(): lax.all_to_all(grads.reshape(outgoing.shape), 'tensor', split_axis=0, con...  9.33 us
    pallas_call x1, Pallas kernels, attend(): pl.pallas_call(attention_kernel, in_specs=[VMEM, VMEM, HBM, HBM], out_spe...  7.37 us
    pallas_call x1, Pallas kernels, finish(): pl.pallas_call(finish_kernel, in_specs=[SMEM, VMEM, VMEM, HBM], out_specs...  3.33 us
    pallas_call x1, Pallas kernels, pack(): pl.pallas_call(pack_kernel, in_specs=[HBM] * 3, out_specs=HBM, out_shape=...  2.39 us
  transfers between devices with their start and end apart: 4, of which 2 were waited for; matrix products, arithmetic and copies ran while one was open for 0% of the time, Pallas kernels for 4%

profile of v3, /device:TPU:1, one launch (start us, length us, event | category | flops | bytes accessed | tf_op | source)
XLA Modules:
  0.0 116.5 jit_solution(7343770166821248124)
XLA Ops:
  0.6 2.4 %pack_rows.1 = bf16[8,64,1280]{2,1,0:T(8,128)(2,1)} custom-call(bf16[64,8192]{1,0:T(8,128)(2,1)} %q_ref.1, bf16[64,1024]{1,0:T(8,128)(2,1)} %k_ref.1, bf16[64,1024]{1,0:T(8,128)(2,1)} %v_ref.1), custom_call_target="tpu_custom_call" | custom-call | bytes 2621440 | tf_op jit(solution)/shard_map/pack_rows/pallas_call | solution.py:75
  3.0 0.0 copy-start.2
  3.0 0.0 copy-start
  3.1 0.0 copy-start.1
  3.1 0.0 copy-start.3
  3.1 0.0 copy-start.4
  3.1 10.3 %all-to-all-start = ((bf16[8,64,1280]{2,1,0:T(8,128)(2,1)}), bf16[8,64,1280]{2,1,0:T(8,128)(2,1)S(1)}, u32[]{:S(2)}, u32[]{:S(2)}) async-start(bf16[8,64,1280]{2,1,0:T(8,128)(2,1)} %pack_rows.1), calls=%async_computation | async-start | bytes 2621440 | tf_op jit(solution)/shard_map/all_to_all | solution.py:374
  13.3 0.0 copy-done.2
  13.4 0.0 copy-done
  13.4 0.0 copy-done.1
  13.4 0.0 copy-done.3
  13.4 1.2 %layout.1 = (bf16[128,1024]{1,0:T(8,128)(2,1)S(1)}, s32[8,512]{1,0:T(8,128)S(1)}, s32[1]{0:T(128)}) custom-call(s32[1]{0:T(128)} %bitcast.group_ref, s32[64]{0:T(128)S(1)} %copy-done.2, s32[64]{0:T(128)S(1)} %copy-done.3, s32[64]{0:T(128)S(1)} %copy-done.4, s32[64,512]{1,0:T(8,128)S(1)} %copy-done.1, bf16[512,1024]{1,0:T(8,128)(2,1)S(1)} %copy-done), custom_call_target="tpu_custom_call" | custom-call | flops 134217728 | bytes 1048576 | tf_op jit(solution)/shard_map/layout/pallas_call | solution.py:158
  14.6 43.3 %conditional.2 = (bf16[128,1024]{1,0:T(8,128)(2,1)}) conditional(s32[]{:T(128)} %bitcast.1, bf16[128,1024]{1,0:T(8,128)(2,1)S(1)} %get-tuple-element.269, bf16[128,1024]{1,0:T(8,128)(2,1)S(1)} %get-tuple-element.269, bf16[128,1024]{1,0:T(8,128)(2,1)S(1)} %get-tuple-element.269, ...), branch_computations={%region_0.0_spmd, %region_1.0_spmd, %region_2.0_spmd, %region_3.0_... | conditional | bytes 1048624 | solution.py:365
  14.7 8.6 %collective-permute-start.26 = (bf16[128,1024]{1,0:T(8,128)(2,1)S(1)}, bf16[128,1024]{1,0:T(8,128)(2,1)}, u32[]{:S(2)}, u32[]{:S(2)}) collective-permute-start(bf16[128,1024]{1,0:T(8,128)(2,1)S(1)} %param.26), channel_id=1, source_target_pairs={{0,216},{8,208},{16,200},{24,192},{32,248},{40,240},{48,232},{56,2... | collective-permute-start | bytes 786440 | tf_op jit(solution)/shard_map/cond/branch_26_fun/ppermute | solution.py:363
  23.3 34.7 %collective-permute-done.26 = bf16[128,1024]{1,0:T(8,128)(2,1)} collective-permute-done((bf16[128,1024]{1,0:T(8,128)(2,1)S(1)}, bf16[128,1024]{1,0:T(8,128)(2,1)}, u32[]{:S(2)}, u32[]{:S(2)}) %collective-permute-start.26) | collective-permute-done | bytes 262176 | tf_op jit(solution)/shard_map/cond/branch_26_fun/ppermute | solution.py:363
  57.9 0.0 all-to-all-done
  57.9 7.4 %attention.1 = (bf16[512,1024]{1,0:T(8,128)(2,1)}, bf16[128,1024]{1,0:T(8,128)(2,1)S(1)}, bf16[512,1280]{1,0:T(8,128)(2,1)}) custom-call(bf16[512,1280]{1,0:T(8,128)(2,1)S(1)} %bitcast.5, s32[8,512]{1,0:T(8,128)S(1)} %get-tuple-element.268.facts_ref, bf16[128,1024]{1,0:T(8,128)(2,1)} %get-tuple-element.276.packet_hbm, bf16[512,1024]{1,0:T(8,128)(2,1)S(1)} %copy-done), custom_call_target="tpu_custom_call" | custom-call | flops 3221225472 | bytes 8388608 | tf_op jit(solution)/shard_map/attention/pallas_call | solution.py:327
  65.3 9.3 %all-to-all-start.1 = ((bf16[8,64,1280]{2,1,0:T(8,128)(2,1)}), bf16[8,64,1280]{2,1,0:T(8,128)(2,1)S(1)}, u32[]{:S(2)}, u32[]{:S(2)}) async-start(bf16[8,64,1280]{2,1,0:T(8,128)(2,1)} %bitcast.3), calls=%async_computation.1 | async-start | bytes 2621440 | tf_op jit(solution)/shard_map/all_to_all | solution.py:381
  74.7 37.1 %conditional.3 = (bf16[128,1024]{1,0:T(8,128)(2,1)}) conditional(s32[]{:T(128)} %bitcast.1, bf16[128,1024]{1,0:T(8,128)(2,1)S(1)} %get-tuple-element.270, bf16[128,1024]{1,0:T(8,128)(2,1)S(1)} %get-tuple-element.270, bf16[128,1024]{1,0:T(8,128)(2,1)S(1)} %get-tuple-element.270, ...), branch_computations={%region_63.0_spmd, %region_64.0_spmd, %region_65.0_spmd, %region_6... | conditional | bytes 1048624 | solution.py:365
  74.7 1.9 %collective-permute-start.89 = (bf16[128,1024]{1,0:T(8,128)(2,1)S(1)}, bf16[128,1024]{1,0:T(8,128)(2,1)}, u32[]{:S(2)}, u32[]{:S(2)}) collective-permute-start(bf16[128,1024]{1,0:T(8,128)(2,1)S(1)} %param.89), channel_id=1, source_target_pairs={{0,216},{8,208},{16,200},{24,192},{32,248},{40,240},{48,232},{56,2... | collective-permute-start | bytes 786440 | tf_op jit(solution)/shard_map/cond/branch_26_fun/ppermute | solution.py:363
  76.6 35.1 %collective-permute-done.89 = bf16[128,1024]{1,0:T(8,128)(2,1)} collective-permute-done((bf16[128,1024]{1,0:T(8,128)(2,1)S(1)}, bf16[128,1024]{1,0:T(8,128)(2,1)}, u32[]{:S(2)}, u32[]{:S(2)}) %collective-permute-start.89) | collective-permute-done | bytes 262176 | tf_op jit(solution)/shard_map/cond/branch_26_fun/ppermute | solution.py:363
  111.7 3.3 %finish_out.1 = bf16[512,1024]{1,0:T(8,128)(2,1)} custom-call(s32[1]{0:T(128)} %get-tuple-element.267.live_ref, s32[8,512]{1,0:T(8,128)S(1)} %get-tuple-element.268.facts_ref, bf16[128,1024]{1,0:T(8,128)(2,1)} %get-tuple-element.277.packet_ref, bf16[512,1024]{1,0:T(8,128)(2,1)} %get-tuple-element.271.out_ref), custom_call_target="tpu_custom_call", output_to_operand_aliasing={{}: (3, {})} | custom-call | flops 33554432 | bytes 1048576 | tf_op jit(solution)/shard_map/finish_out/pallas_call | solution.py:196
  115.1 0.0 all-to-all-done.1.packed_ref
  115.1 1.2 %unpack_rows.1 = (bf16[64,8192]{1,0:T(8,128)(2,1)}, bf16[64,1024]{1,0:T(8,128)(2,1)}, bf16[64,1024]{1,0:T(8,128)(2,1)}) custom-call(bf16[8,64,1280]{2,1,0:T(8,128)(2,1)S(1)} %all-to-all-done.1.packed_ref), custom_call_target="tpu_custom_call" | custom-call | bytes 2621440 | tf_op jit(solution)/shard_map/unpack_rows/pallas_call | solution.py:110
  (1 shorter events, 0.0 us)
Async XLA Ops:
  3.0 10.3 %copy-start.2 = (s32[64]{0:T(128)S(1)}, s32[64]{0:T(128)}, u32[]{:S(2)}) copy-start(s32[64]{0:T(128)} %mask_ref.1) | copy-start | bytes 772
  3.0 10.4 %copy-start = (bf16[512,1024]{1,0:T(8,128)(2,1)S(1)}, bf16[512,1024]{1,0:T(8,128)(2,1)}, u32[]{:S(2)}) copy-start(bf16[512,1024]{1,0:T(8,128)(2,1)} %grad_hbm.1) | copy-start | bytes 3145732
  3.1 10.3 %copy-start.1 = (s32[64,512]{1,0:T(8,128)S(1)}, s32[64,512]{1,0:T(8,128)}, u32[]{:S(2)}) copy-start(s32[64,512]{1,0:T(8,128)} %seg_ref.1) | copy-start | bytes 393220
  3.1 10.3 %copy-start.3 = (s32[64]{0:T(128)S(1)}, s32[64]{0:T(128)}, u32[]{:S(2)}) copy-start(s32[64]{0:T(128)} %sender_ref.1) | copy-start | bytes 772
  3.1 10.3 %copy-start.4 = (s32[64]{0:T(128)S(1)}, s32[64]{0:T(128)}, u32[]{:S(2)}) copy-start(s32[64]{0:T(128)} %moved_ref.1) | copy-start | bytes 772
  3.1 54.9 %all-to-all-start = ((bf16[8,64,1280]{2,1,0:T(8,128)(2,1)}), bf16[8,64,1280]{2,1,0:T(8,128)(2,1)S(1)}, u32[]{:S(2)}, u32[]{:S(2)}) async-start(bf16[8,64,1280]{2,1,0:T(8,128)(2,1)} %pack_rows.1), calls=%async_computation | async-start | bytes 2621440 | tf_op jit(solution)/shard_map/all_to_all | solution.py:374
  14.7 43.3 %collective-permute-start.26 = (bf16[128,1024]{1,0:T(8,128)(2,1)S(1)}, bf16[128,1024]{1,0:T(8,128)(2,1)}, u32[]{:S(2)}, u32[]{:S(2)}) collective-permute-start(bf16[128,1024]{1,0:T(8,128)(2,1)S(1)} %param.26), channel_id=1, source_target_pairs={{0,216},{8,208},{16,200},{24,192},{32,248},{40,240},{48,232},{56,2... | collective-permute-start | bytes 786440 | tf_op jit(solution)/shard_map/cond/branch_26_fun/ppermute | solution.py:363
  65.3 49.7 %all-to-all-start.1 = ((bf16[8,64,1280]{2,1,0:T(8,128)(2,1)}), bf16[8,64,1280]{2,1,0:T(8,128)(2,1)S(1)}, u32[]{:S(2)}, u32[]{:S(2)}) async-start(bf16[8,64,1280]{2,1,0:T(8,128)(2,1)} %bitcast.3), calls=%async_computation.1 | async-start | bytes 2621440 | tf_op jit(solution)/shard_map/all_to_all | solution.py:381
  74.7 37.1 %collective-permute-start.89 = (bf16[128,1024]{1,0:T(8,128)(2,1)S(1)}, bf16[128,1024]{1,0:T(8,128)(2,1)}, u32[]{:S(2)}, u32[]{:S(2)}) collective-permute-start(bf16[128,1024]{1,0:T(8,128)(2,1)S(1)} %param.89), channel_id=1, source_target_pairs={{0,216},{8,208},{16,200},{24,192},{32,248},{40,240},{48,232},{56,2... | collective-permute-start | bytes 786440 | tf_op jit(solution)/shard_map/cond/branch_26_fun/ppermute | solution.py:363
